TPU v7x, 32 devices: a whole 2x2x4 slice. The times are simulated.
32 devices in a mesh: seq: 4 (over x, core), fsdp: 8 (over z, y).
Axes of the slice: x: 2, y: 2, z: 4, core: 2. Of those that a mesh axis runs over, the one named last changes fastest.
Arguments:
- inputs: bfloat16 [8, 4096, 1024], P('fsdp', 'seq'), may hold values from -6 to 6
- g_attn: bfloat16 [1024], P('fsdp'), may hold values from 0.5 to 1.5
- w_query: bfloat16 [1024, 1024], P('fsdp'), may hold values from -0.1875 to 0.1875
- w_key: bfloat16 [1024, 1024], P('fsdp'), may hold values from -0.1875 to 0.1875
- w_value: bfloat16 [1024, 1024], P('fsdp'), may hold values from -0.1875 to 0.1875
- w_beta: bfloat16 [1024, 8], P('fsdp'), may hold values from -0.1875 to 0.1875
- conv_taps: bfloat16 [4, 3072], P(None, 'fsdp'), may hold values from -3 to 3
- o_gain: bfloat16 [128], P('fsdp'), may hold values from 0.5 to 1.5
- w_out: bfloat16 [1024, 1024], P('fsdp'), may hold values from -0.1875 to 0.1875
- g_mlp: bfloat16 [1024], P('fsdp'), may hold values from 0.5 to 1.5
- w_gate: bfloat16 [1024, 2816], P('fsdp'), may hold values from -0.1875 to 0.1875
- w_up: bfloat16 [1024, 2816], P('fsdp'), may hold values from -0.1875 to 0.1875
- w_down: bfloat16 [2816, 1024], P(None, 'fsdp'), may hold values from -0.109375 to 0.109375
- cotangent: bfloat16 [8, 4096, 1024], P('fsdp', 'seq'), may hold values from -6 to 6
Outputs:
- layer_out: bfloat16 [8, 4096, 1024], P('fsdp', 'seq')
- grad_inputs: float32 [8, 4096, 1024], P('fsdp', 'seq')
- grad_g_attn: float32 [1024], P('fsdp')
- grad_w_query: float32 [1024, 1024], P('fsdp')
- grad_w_key: float32 [1024, 1024], P('fsdp')
- grad_w_value: float32 [1024, 1024], P('fsdp')
- grad_w_beta: float32 [1024, 8], P('fsdp')
- grad_conv_taps: float32 [4, 3072], P(None, 'fsdp')
- grad_o_gain: float32 [128], P('fsdp')
- grad_w_out: float32 [1024, 1024], P('fsdp')
- grad_g_mlp: float32 [1024], P('fsdp')
- grad_w_gate: float32 [1024, 2816], P('fsdp')
- grad_w_up: float32 [1024, 2816], P('fsdp')
- grad_w_down: float32 [2816, 1024], P(None, 'fsdp')
All inputs are finite; a program needn't handle non-finite values.
Results may differ from a plain program's by a relative error of at most 0.017.
Values may be sent and summed in bfloat16 or wider, within the bound.
A program may use at most 256 MiB of HBM per device.

v0:
```python
import jax
import jax.numpy as jnp
from jax import lax
from jax.sharding import PartitionSpec as P

BLOCK = 64


highest = lax.Precision.HIGHEST
epsilon = 1e-06


def rms_scale(values, gain_vec):
    return (
        values * lax.rsqrt(jnp.mean(values * values, axis=-1, keepdims=True) + epsilon) * gain_vec
    )


def transposed_by(left_side, right_side):
    return lax.dot_general(
        left_side, right_side, (((0,), (0,)), ((), ())), preferred_element_type=jnp.float32
    )


def by_transposed(left_side, right_side):
    return lax.dot_general(
        left_side, right_side, (((1,), (1,)), ((), ())), preferred_element_type=jnp.float32
    )


def norm_backward(values, gain_vec, grad_out):
    scaling = lax.rsqrt(jnp.mean(values * values, axis=-1, keepdims=True) + epsilon)
    unit_rows = values * scaling
    gain_grad = jnp.sum(grad_out * unit_rows, axis=0)
    scaled_grad = grad_out * gain_vec
    input_grad = scaling * (
        scaled_grad - unit_rows * jnp.mean(scaled_grad * unit_rows, axis=-1, keepdims=True)
    )
    return (input_grad, gain_grad)


def unit_inverse(strict_lower):
    width_all = strict_lower.shape[-1]
    identity = jnp.eye(width_all, dtype=jnp.float32)
    result = identity - strict_lower
    powered = strict_lower
    for doubling in range(1, (width_all - 1).bit_length()):
        powered = jnp.einsum("gij,gjk->gik", powered, powered, precision=highest)
        result = jnp.einsum("gij,gjk->gik", result, identity + powered, precision=highest)
    return result


def causal_conv(signal, conv_weights):
    length = signal.shape[0]
    padded = jnp.pad(signal, ((conv_weights.shape[0] - 1, 0), (0, 0), (0, 0)))
    summed_taps = conv_weights[0] * padded[0:length]
    for offset in range(1, conv_weights.shape[0]):
        summed_taps = summed_taps + conv_weights[offset] * padded[offset : offset + length]
    return jax.nn.silu(summed_taps)


def block_step(memory, pieces):
    queries, key_rows, values, beta_rates = pieces
    scaling = queries.shape[-1] ** (-0.5)
    keys_rated = key_rows * beta_rates[..., None]
    values_rated = values * beta_rates[..., None]
    products = beta_rates[..., None] * jnp.einsum("gie,gje->gij", key_rows, key_rows)
    inverse = unit_inverse(jnp.tril(products, -1))
    weights_wy = jnp.einsum("gij,gje->gie", inverse, keys_rated, precision=highest)
    targets = jnp.einsum("gij,gje->gie", inverse, values_rated, precision=highest)
    fresh = targets - jnp.einsum("gie,gef->gif", weights_wy, memory, precision=highest)
    scores = jnp.tril(jnp.einsum("gie,gje->gij", queries, key_rows))
    output = scaling * (
        jnp.einsum("gie,gef->gif", queries, memory, precision=highest)
        + jnp.einsum("gij,gjf->gif", scores, fresh, precision=highest)
    )
    memory = memory + jnp.einsum("gie,gif->gef", key_rows, fresh, precision=highest)
    return (memory, output)


def prepare(queries, key_rows, values, logits, conv_weights):
    queries = causal_conv(queries, conv_weights[:, 0])
    key_rows = causal_conv(key_rows, conv_weights[:, 1])
    values = causal_conv(values, conv_weights[:, 2])
    queries = queries * lax.rsqrt(jnp.sum(queries * queries, axis=-1, keepdims=True) + epsilon)
    key_rows = key_rows * lax.rsqrt(jnp.sum(key_rows * key_rows, axis=-1, keepdims=True) + epsilon)
    return (queries, key_rows, values, jax.nn.sigmoid(logits))


def recurrence(queries, key_rows, values, beta_rates, gain_vec):
    length, head_count, head_size = queries.shape
    block_count = length // BLOCK

    def blocks(array):
        return jnp.moveaxis(array.reshape((block_count, BLOCK) + array.shape[1:]), 2, 1)

    initial = jnp.zeros((head_count, head_size, head_size), jnp.float32)
    final_memory, outputs = lax.scan(
        jax.checkpoint(block_step),
        initial,
        (blocks(queries), blocks(key_rows), blocks(values), blocks(beta_rates)),
    )
    outputs = jnp.moveaxis(outputs, 1, 2).reshape(length, head_count, head_size)
    return rms_scale(outputs, gain_vec)


def rounded(values):
    return lax.optimization_barrier(values.astype(jnp.bfloat16)).astype(jnp.float32)


def local(
    inputs,
    g_attn,
    w_query,
    w_key,
    w_value,
    w_beta,
    conv_taps,
    o_gain,
    w_out,
    g_mlp,
    w_gate,
    w_up,
    w_down,
    cotangent,
):
    mixer_full = (
        lax.all_gather(g_attn, "fsdp", axis=0, tiled=True),
        lax.all_gather(w_query, "fsdp", axis=0, tiled=True),
        lax.all_gather(w_key, "fsdp", axis=0, tiled=True),
        lax.all_gather(w_value, "fsdp", axis=0, tiled=True),
        lax.all_gather(w_beta, "fsdp", axis=0, tiled=True),
        lax.all_gather(conv_taps, "fsdp", axis=1, tiled=True),
        lax.all_gather(o_gain, "fsdp", axis=0, tiled=True),
        lax.all_gather(w_out, "fsdp", axis=0, tiled=True),
    )
    dense_full = (
        lax.all_gather(g_mlp, "fsdp", axis=0, tiled=True),
        lax.all_gather(w_gate, "fsdp", axis=0, tiled=True),
        lax.all_gather(w_up, "fsdp", axis=0, tiled=True),
        lax.all_gather(w_down, "fsdp", axis=1, tiled=True),
    )
    groups = lax.axis_size("seq")
    position = lax.axis_index("seq")
    tokens = inputs[0].astype(jnp.float32)
    rows_here = tokens.shape[0]
    head_count = mixer_full[4].shape[1]
    head_size = mixer_full[6].shape[0]
    width_all = head_count * head_size
    per_device = head_count // groups
    tap_count = mixer_full[5].shape[0]
    gain_attn = mixer_full[0].astype(jnp.float32)
    normed = rms_scale(tokens, gain_attn).astype(jnp.bfloat16)

    def project(matrix):
        return (
            jnp.dot(normed, matrix, preferred_element_type=jnp.float32)
            .astype(jnp.bfloat16)
            .reshape(rows_here, head_count, head_size)
        )

    query_send = project(mixer_full[1])
    key_send = project(mixer_full[2])
    value_send = project(mixer_full[3])
    logit_send = jnp.dot(normed, mixer_full[4], preferred_element_type=jnp.float32).astype(
        jnp.bfloat16
    )
    query_heads, key_heads, value_heads, logit_heads = (
        lax.all_to_all(query_send, "seq", split_axis=1, concat_axis=0, tiled=True),
        lax.all_to_all(key_send, "seq", split_axis=1, concat_axis=0, tiled=True),
        lax.all_to_all(value_send, "seq", split_axis=1, concat_axis=0, tiled=True),
        lax.all_to_all(logit_send, "seq", split_axis=1, concat_axis=0, tiled=True),
    )
    taps_all = mixer_full[5].astype(jnp.float32).reshape(tap_count, 3, head_count, head_size)
    taps_here = lax.dynamic_slice_in_dim(taps_all, position * per_device, per_device, 2)
    gain_out = mixer_full[6].astype(jnp.float32)
    prepared, prepare_pull = jax.vjp(
        prepare,
        query_heads.astype(jnp.float32),
        key_heads.astype(jnp.float32),
        value_heads.astype(jnp.float32),
        logit_heads.astype(jnp.float32),
        taps_here,
    )
    unit_query, unit_key, conv_value, beta_rates = prepared
    mixed_heads, recurrence_pull = jax.vjp(
        recurrence,
        rounded(unit_query),
        rounded(unit_key),
        rounded(conv_value),
        beta_rates,
        gain_out,
    )
    returned = lax.all_to_all(
        mixed_heads.astype(jnp.bfloat16), "seq", split_axis=0, concat_axis=1, tiled=True
    )
    head_rows = returned.reshape(rows_here, width_all)
    attended = tokens + jnp.dot(head_rows, mixer_full[7], preferred_element_type=jnp.float32)
    gain_mlp = dense_full[0].astype(jnp.float32)
    normed_ff = rms_scale(attended, gain_mlp).astype(jnp.bfloat16)
    gated = jnp.dot(normed_ff, dense_full[1], preferred_element_type=jnp.float32)
    upward = jnp.dot(normed_ff, dense_full[2], preferred_element_type=jnp.float32)
    sigmoid_gate = jax.nn.sigmoid(gated)
    activated = gated * sigmoid_gate
    hidden = (activated * upward).astype(jnp.bfloat16)
    layer_out = (
        attended + jnp.dot(hidden, dense_full[3], preferred_element_type=jnp.float32)
    ).astype(jnp.bfloat16)
    dense_back = (
        lax.all_gather(g_mlp, "fsdp", axis=0, tiled=True),
        lax.all_gather(w_gate, "fsdp", axis=0, tiled=True),
        lax.all_gather(w_up, "fsdp", axis=0, tiled=True),
        lax.all_gather(w_down, "fsdp", axis=1, tiled=True),
    )
    grad_out = cotangent[0]
    grad_down = transposed_by(hidden, grad_out)
    grad_hidden = by_transposed(grad_out, dense_back[3])
    grad_gate = (grad_hidden * upward * sigmoid_gate * (1.0 + gated * (1.0 - sigmoid_gate))).astype(
        jnp.bfloat16
    )
    grad_upward = (grad_hidden * activated).astype(jnp.bfloat16)
    grad_gate_matrix = transposed_by(normed_ff, grad_gate)
    grad_up_matrix = transposed_by(normed_ff, grad_upward)
    grad_normed_ff = by_transposed(grad_gate, dense_back[1]) + by_transposed(
        grad_upward, dense_back[2]
    )
    grad_from_ff, grad_gain_mlp = norm_backward(attended, gain_mlp, grad_normed_ff)
    grad_attended = grad_out.astype(jnp.float32) + grad_from_ff
    mixer_back = (
        lax.all_gather(g_attn, "fsdp", axis=0, tiled=True),
        lax.all_gather(w_query, "fsdp", axis=0, tiled=True),
        lax.all_gather(w_key, "fsdp", axis=0, tiled=True),
        lax.all_gather(w_value, "fsdp", axis=0, tiled=True),
        lax.all_gather(w_beta, "fsdp", axis=0, tiled=True),
        lax.all_gather(conv_taps, "fsdp", axis=1, tiled=True),
        lax.all_gather(o_gain, "fsdp", axis=0, tiled=True),
        lax.all_gather(w_out, "fsdp", axis=0, tiled=True),
    )
    grad_mixed = grad_attended.astype(jnp.bfloat16)
    grad_out_matrix = transposed_by(head_rows, grad_mixed)
    grad_head_send = (
        by_transposed(grad_mixed, mixer_back[7])
        .astype(jnp.bfloat16)
        .reshape(rows_here, head_count, head_size)
    )
    grad_head_rows = lax.all_to_all(grad_head_send, "seq", split_axis=1, concat_axis=0, tiled=True)
    grad_unit_query, grad_unit_key, grad_conv_value, grad_rates, grad_gain_out = recurrence_pull(
        grad_head_rows.astype(jnp.float32)
    )
    grad_query, grad_key, grad_value, grad_logits, grad_taps_here = prepare_pull(
        (grad_unit_query, grad_unit_key, grad_conv_value, grad_rates)
    )
    query_back, key_back, value_back, logit_back = (
        lax.all_to_all(
            grad_query.astype(jnp.bfloat16), "seq", split_axis=0, concat_axis=1, tiled=True
        ),
        lax.all_to_all(
            grad_key.astype(jnp.bfloat16), "seq", split_axis=0, concat_axis=1, tiled=True
        ),
        lax.all_to_all(
            grad_value.astype(jnp.bfloat16), "seq", split_axis=0, concat_axis=1, tiled=True
        ),
        lax.all_to_all(
            grad_logits.astype(jnp.bfloat16), "seq", split_axis=0, concat_axis=1, tiled=True
        ),
    )
    query_back = query_back.reshape(rows_here, width_all)
    key_back = key_back.reshape(rows_here, width_all)
    value_back = value_back.reshape(rows_here, width_all)
    grad_query_matrix = transposed_by(normed, query_back)
    grad_key_matrix = transposed_by(normed, key_back)
    grad_value_matrix = transposed_by(normed, value_back)
    grad_beta_matrix = transposed_by(normed, logit_back)
    grad_normed = (
        by_transposed(query_back, mixer_back[1])
        + by_transposed(key_back, mixer_back[2])
        + by_transposed(value_back, mixer_back[3])
        + by_transposed(logit_back, mixer_back[4])
    )
    grad_from_attn, grad_gain_attn = norm_backward(tokens, gain_attn, grad_normed)
    grad_inputs = (grad_attended + grad_from_attn)[None]
    taps_blank = jnp.zeros((tap_count, 3, head_count, head_size), jnp.float32)
    grad_taps = lax.dynamic_update_slice_in_dim(
        taps_blank, grad_taps_here, position * per_device, 2
    ).reshape(tap_count, 3 * width_all)
    shards = (
        lax.psum_scatter(grad_gain_attn, "fsdp", scatter_dimension=0, tiled=True),
        lax.psum_scatter(grad_query_matrix, "fsdp", scatter_dimension=0, tiled=True),
        lax.psum_scatter(grad_key_matrix, "fsdp", scatter_dimension=0, tiled=True),
        lax.psum_scatter(grad_value_matrix, "fsdp", scatter_dimension=0, tiled=True),
        lax.psum_scatter(grad_beta_matrix, "fsdp", scatter_dimension=0, tiled=True),
        lax.psum_scatter(grad_taps, "fsdp", scatter_dimension=1, tiled=True),
        lax.psum_scatter(grad_gain_out, "fsdp", scatter_dimension=0, tiled=True),
        lax.psum_scatter(grad_out_matrix, "fsdp", scatter_dimension=0, tiled=True),
        lax.psum_scatter(grad_gain_mlp, "fsdp", scatter_dimension=0, tiled=True),
        lax.psum_scatter(grad_gate_matrix, "fsdp", scatter_dimension=0, tiled=True),
        lax.psum_scatter(grad_up_matrix, "fsdp", scatter_dimension=0, tiled=True),
        lax.psum_scatter(grad_down, "fsdp", scatter_dimension=1, tiled=True),
    )
    summed = (
        lax.psum(shards[0].astype(jnp.bfloat16), "seq").astype(jnp.float32),
        lax.psum(shards[1].astype(jnp.bfloat16), "seq").astype(jnp.float32),
        lax.psum(shards[2].astype(jnp.bfloat16), "seq").astype(jnp.float32),
        lax.psum(shards[3].astype(jnp.bfloat16), "seq").astype(jnp.float32),
        lax.psum(shards[4].astype(jnp.bfloat16), "seq").astype(jnp.float32),
        lax.psum(shards[5].astype(jnp.bfloat16), "seq").astype(jnp.float32),
        lax.psum(shards[6].astype(jnp.bfloat16), "seq").astype(jnp.float32),
        lax.psum(shards[7].astype(jnp.bfloat16), "seq").astype(jnp.float32),
        lax.psum(shards[8].astype(jnp.bfloat16), "seq").astype(jnp.float32),
        lax.psum(shards[9].astype(jnp.bfloat16), "seq").astype(jnp.float32),
        lax.psum(shards[10].astype(jnp.bfloat16), "seq").astype(jnp.float32),
        lax.psum(shards[11].astype(jnp.bfloat16), "seq").astype(jnp.float32),
    )
    return (
        layer_out[None],
        grad_inputs,
        summed[0],
        summed[1],
        summed[2],
        summed[3],
        summed[4],
        summed[5],
        summed[6],
        summed[7],
        summed[8],
        summed[9],
        summed[10],
        summed[11],
    )


def solution(mesh):
    placed = (
        P("fsdp", "seq", None),
        P("fsdp"),
        P("fsdp", None),
        P("fsdp", None),
        P("fsdp", None),
        P("fsdp", None),
        P(None, "fsdp"),
        P("fsdp"),
        P("fsdp", None),
        P("fsdp"),
        P("fsdp", None),
        P("fsdp", None),
        P(None, "fsdp"),
        P("fsdp", "seq", None),
    )
    return jax.shard_map(
        local,
        mesh=mesh,
        in_specs=placed,
        out_specs=(
            P("fsdp", "seq", None),
            P("fsdp", "seq", None),
            P("fsdp"),
            P("fsdp", None),
            P("fsdp", None),
            P("fsdp", None),
            P("fsdp", None),
            P(None, "fsdp"),
            P("fsdp"),
            P("fsdp", None),
            P("fsdp"),
            P("fsdp", None),
            P("fsdp", None),
            P(None, "fsdp"),
        ),
        check_vma=False,
    )
```

profile of v0, /device:TPU:0, one launch (start us, length us, event | category | flops | bytes accessed | tf_op | source)
XLA Modules:
  0.0 3516.2 jit_solution(16501139935440440826)
XLA Ops:
  14.1 22.2 all-gather
  36.2 26.3 all_gather.47
  82.4 30.6 all_gather.44
  114.6 17.3 all-reduce.30
  131.8 6.1 convolution_convert_fusion.1
  147.0 15.7 all-gather.10.cloned.1.call-done
  162.8 6.1 convolution_convert_fusion.3
  187.0 13.1 multiply_reduce_fusion.18
  222.1 669.9 %while.42 = (s32[]{:T(128)}, f32[2,128,128]{2,1,0:T(8,128)S(1)}, f32[64,2,64,128]{3,2,0,1:T(8,128)}, f32[64,2,128,128]{3,2,1,0:T(8,128)}, f32[64,2,64,128]{3,2,1...) while((s32[]{:T(128)}, f32[2,128,128]{2,1,0:T(8,128)S(1)}, ...), condition=%wide.region_4.5_spmd.clone.clone, body=%wide.region_3.4_spmd.clone.clone.sunk | while | flops 180682752 | bytes 2899078 | solution.py:98
  898.5 18.1 copy.338
  921.0 18.0 all-gather.1
  962.4 11.6 fusion.239
  974.0 11.9 fusion.240
  985.9 22.0 multiply_convert_fusion
  1007.9 10.0 fusion.241
  1018.0 9.5 multiply_reduce_fusion.3
  1037.9 25.6 all-to-all-done.5
  1080.6 1232.9 %while.41 = (s32[]{:T(128)}, f32[2,128,128]{2,1,0:T(8,128)S(1)}, f32[64,2,64,128]{3,2,0,1:T(8,128)}, f32[64,2,64,128]{3,2,0,1:T(8,128)}, f32[64,2,64,128]{3,2,0,...) while((s32[]{:T(128)}, f32[2,128,128]{2,1,0:T(8,128)S(1)}, ...), condition=%wide.region_13.14_spmd.clone, body=%wide.region_9.13_spmd.clone.sunk | while | flops 478969792 | bytes 9755335 | solution.py:98
  2319.5 7.7 multiply_reduce_fusion.10
  2339.4 12.2 multiply_reduce_fusion.14
  2354.9 7.2 fusion.187
  2362.7 6.6 broadcast_multiply_fusion.8
  2374.2 17.8 copy.357
  2392.0 28.9 all_to_all.125
  2426.5 5.9 fusion.209
  2433.1 6.6 broadcast_multiply_fusion
  2444.5 17.8 copy.353
  2462.4 28.2 all_to_all.126
  2496.1 6.0 fusion.211
  2502.8 6.7 broadcast_multiply_fusion.4
  2514.5 17.8 copy.363
  2532.3 28.6 all_to_all.127
  2566.4 5.9 fusion.207
  2572.4 12.1 fusion.242
  2584.7 11.9 fusion.243
  2596.6 11.9 fusion.183
  2609.9 11.8 fusion.181
  2627.4 6.8 fusion.245
  2640.4 14.7 reduce-scatter.14.cloned.1.call-done
  2656.9 89.8 %reduce-scatter.12.cloned.1.call-done = f32[128,1024]{1,0:T(8,128)} async-done(((f32[1024,1024]{1,0:T(8,128)}), f32[128,1024]{1,0:T(8,128)}) %reduce-scatter.12.cloned.1.call-update) | async-done | bytes 524304 | tf_op jit(solution)/shard_map/reduce_scatter | solution.py:288
  2748.5 89.7 %reduce-scatter.16.cloned.1.call-done = f32[128,1024]{1,0:T(8,128)} async-done(((f32[1024,1024]{1,0:T(8,128)}), f32[128,1024]{1,0:T(8,128)}) %reduce-scatter.16.cloned.1.call-update) | async-done | bytes 524304 | tf_op jit(solution)/shard_map/reduce_scatter | solution.py:290
  2839.9 194.5 %reduce-scatter.22.cloned.1.call-done = f32[128,2816]{1,0:T(8,128)} async-done(((f32[1024,2816]{1,0:T(8,128)}), f32[128,2816]{1,0:T(8,128)}) %reduce-scatter.22.cloned.1.call-update) | async-done | bytes 1441808 | tf_op jit(solution)/shard_map/reduce_scatter | solution.py:296
  3036.8 193.4 %reduce-scatter.24.cloned.1.call-done = f32[128,2816]{1,0:T(8,128)} async-done(((f32[1024,2816]{1,0:T(8,128)}), f32[128,2816]{1,0:T(8,128)}) %reduce-scatter.24.cloned.1.call-update) | async-done | bytes 1441808 | tf_op jit(solution)/shard_map/reduce_scatter | solution.py:297
  3232.4 193.7 %reduce-scatter.26.cloned.1.call-done = f32[2816,128]{1,0:T(8,128)} async-done(((f32[2816,1024]{1,0:T(8,128)}), f32[2816,128]{1,0:T(8,128)}) %reduce-scatter.26.cloned.1.call-update) | async-done | bytes 1441808 | tf_op jit(solution)/shard_map/reduce_scatter | solution.py:298
  3436.7 35.1 all-reduce.34
  3472.1 6.4 all-reduce.35
  3481.2 6.6 fusion.156
  3493.2 7.0 all-reduce.39.cloned.1.call-done
  (5907 shorter events, 2108.9 us)
Async XLA Ops:
  7.2 29.0 copy-start.72
  7.2 60.4 %all-gather.12.cloned.1.call-start = ((), (), s32[]{:S(2)}) async-start(), calls=%async_computation.20 | async-start | bytes 2359296 | tf_op jit(solution)/shard_map/all_gather | solution.py:131
  7.9 123.9 %all-gather.14.cloned.1.call-start = ((), (), s32[]{:S(2)}) async-start(), calls=%async_computation.21 | async-start | bytes 2359296 | tf_op jit(solution)/shard_map/all_gather | solution.py:129
  8.7 154.1 %all-gather.10.cloned.1.call-start = ((), (), s32[]{:S(2)}) async-start(), calls=%async_computation.19 | async-start | bytes 2359296 | tf_op jit(solution)/shard_map/all_gather | solution.py:130
  9.4 944.5 %all-gather.16.cloned.1.call-start = ((), (), s32[]{:S(2)}) async-start(), calls=%async_computation.22 | async-start | bytes 2359296 | tf_op jit(solution)/shard_map/all_gather | solution.py:135
  10.0 951.1 %all-gather.18.cloned.1.call-start = ((), (), s32[]{:S(2)}) async-start(), calls=%async_computation.23 | async-start | bytes 6488064 | tf_op jit(solution)/shard_map/all_gather | solution.py:139
  10.6 963.4 %all-gather.20.cloned.1.call-start = ((), (), s32[]{:S(2)}) async-start(), calls=%async_computation.24 | async-start | bytes 6488064 | tf_op jit(solution)/shard_map/all_gather | solution.py:140
  14.0 59.1 %copy-start.10 = (bf16[1,1024,1024]{1,2,0:T(8,128)(2,1)}, bf16[1,1024,1024]{1,2,0:T(8,128)(2,1)S(1)}, u32[]{:S(2)}) copy-start(bf16[1,1024,1024]{1,2,0:T(8,128)(2,1)S(1)} %copy.325) | copy-start | bytes 6291460
  36.2 126.5 %copy-start.41 = (f32[8,1,128]{2,1,0:T(1,128)}, f32[8,1,128]{2,1,0:T(1,128)S(1)}, u32[]{:S(2)}) copy-start(f32[8,1,128]{2,1,0:T(1,128)S(1)} %convert_element_type.350) | copy-start | bytes 12292
  63.0 99.8 %copy-start.43 = (f32[1024]{0:T(1024)}, f32[1024]{0:T(1024)S(1)}, u32[]{:S(2)}) copy-start(f32[1024]{0:T(1024)S(1)} %add_rsqrt_fusion.3) | copy-start | bytes 12292
  64.4 12.7 all-to-all-start.1
  73.1 39.9 %copy-start.73 = (u32[32]{0:T(128)S(1)}, u32[32]{0:T(128)}, u32[]{:S(2)}) copy-start(u32[32]{0:T(128)} %constant.224) | copy-start | bytes 388
  73.1 41.2 %copy-start.79 = (bf16[16]{0:T(256)(128)(2,1)S(1)}, bf16[16]{0:T(256)(128)(2,1)}, u32[]{:S(2)}) copy-start(bf16[16]{0:T(256)(128)(2,1)} %param.25) | copy-start | bytes 100
  77.1 69.7 %copy-start.37 = (bf16[1024,4,2]{0,2,1:T(2,128)(2,1)}, bf16[1024,4,2]{0,2,1:T(2,128)(2,1)S(1)}, u32[]{:S(2)}) copy-start(bf16[1024,4,2]{0,2,1:T(2,128)(2,1)S(1)} %all-to-all-done.1) | copy-start | bytes 49156
  77.1 64.8 %all-to-all-start.2 = ((bf16[1024,8,128]{2,0,1:T(8,128)(2,1)}), bf16[1024,8,128]{2,0,1:T(8,128)(2,1)}, u32[]{:S(2)}, u32[]{:S(2)}) async-start(bf16[1024,8,128]{2,0,1:T(8,128)(2,1)} %copy.329), calls=%async_computation.2 | async-start | bytes 4194304 | tf_op jit(solution)/shard_map/all_to_all | solution.py:171
  81.6 904.3 %all-gather.22.cloned.1.call-start = ((), (), s32[]{:S(2)}) async-start(), calls=%async_computation.25 | async-start | bytes 6488064 | tf_op jit(solution)/shard_map/all_gather | solution.py:141
  141.9 35.0 all-to-all-start.3
  146.6 39.1 %copy-start.45 = (f32[2,128]{1,0:T(2,128)}, f32[2,128]{1,0:T(2,128)S(1)}, u32[]{:S(2)}) copy-start(f32[2,128]{1,0:T(2,128)S(1)} %get-tuple-element.813) | copy-start | bytes 3076
  146.7 39.1 %copy-start.47 = (f32[2,128]{1,0:T(2,128)}, f32[2,128]{1,0:T(2,128)S(1)}, u32[]{:S(2)}) copy-start(f32[2,128]{1,0:T(2,128)S(1)} %get-tuple-element.814) | copy-start | bytes 3076
  146.7 39.1 %copy-start.49 = (f32[2,128]{1,0:T(2,128)}, f32[2,128]{1,0:T(2,128)S(1)}, u32[]{:S(2)}) copy-start(f32[2,128]{1,0:T(2,128)S(1)} %get-tuple-element.815) | copy-start | bytes 3076
  146.7 39.1 %copy-start.51 = (f32[2,128]{1,0:T(2,128)}, f32[2,128]{1,0:T(2,128)S(1)}, u32[]{:S(2)}) copy-start(f32[2,128]{1,0:T(2,128)S(1)} %get-tuple-element.816) | copy-start | bytes 3076
  146.7 39.1 %copy-start.53 = (f32[2,128]{1,0:T(2,128)}, f32[2,128]{1,0:T(2,128)S(1)}, u32[]{:S(2)}) copy-start(f32[2,128]{1,0:T(2,128)S(1)} %get-tuple-element.810) | copy-start | bytes 3076
  146.7 39.1 %copy-start.55 = (f32[2,128]{1,0:T(2,128)}, f32[2,128]{1,0:T(2,128)S(1)}, u32[]{:S(2)}) copy-start(f32[2,128]{1,0:T(2,128)S(1)} %get-tuple-element.811) | copy-start | bytes 3076
  146.7 39.1 %copy-start.57 = (f32[2,128]{1,0:T(2,128)}, f32[2,128]{1,0:T(2,128)S(1)}, u32[]{:S(2)}) copy-start(f32[2,128]{1,0:T(2,128)S(1)} %get-tuple-element.812) | copy-start | bytes 3076
  146.7 39.1 %copy-start.59 = (f32[2,128]{1,0:T(2,128)}, f32[2,128]{1,0:T(2,128)S(1)}, u32[]{:S(2)}) copy-start(f32[2,128]{1,0:T(2,128)S(1)} %get-tuple-element.821) | copy-start | bytes 3076
  146.7 62.6 %copy-start.61 = (f32[2,128]{1,0:T(2,128)}, f32[2,128]{1,0:T(2,128)S(1)}, u32[]{:S(2)}) copy-start(f32[2,128]{1,0:T(2,128)S(1)} %get-tuple-element.817) | copy-start | bytes 3076
  146.7 62.6 %copy-start.63 = (f32[2,128]{1,0:T(2,128)}, f32[2,128]{1,0:T(2,128)S(1)}, u32[]{:S(2)}) copy-start(f32[2,128]{1,0:T(2,128)S(1)} %get-tuple-element.818) | copy-start | bytes 3076
  146.8 62.6 %copy-start.65 = (f32[2,128]{1,0:T(2,128)}, f32[2,128]{1,0:T(2,128)S(1)}, u32[]{:S(2)}) copy-start(f32[2,128]{1,0:T(2,128)S(1)} %get-tuple-element.819) | copy-start | bytes 3076
  146.8 62.6 %copy-start.67 = (f32[2,128]{1,0:T(2,128)}, f32[2,128]{1,0:T(2,128)S(1)}, u32[]{:S(2)}) copy-start(f32[2,128]{1,0:T(2,128)S(1)} %get-tuple-element.820) | copy-start | bytes 3076
  177.0 30.2 all-to-all-start
  898.4 22.6 copy-start.75
  898.4 40.6 %copy-start.20 = (bf16[1,1024,1024]{2,1,0:T(8,128)(2,1)S(1)}, bf16[1,1024,1024]{2,1,0:T(8,128)(2,1)}, u32[]{:S(2)}) copy-start(bf16[1,1024,1024]{2,1,0:T(8,128)(2,1)} %param.31) | copy-start | bytes 6291460
  916.6 30.2 all-to-all-start.4
  1033.8 29.7 all-to-all-start.5
  1080.6 1237.8 %copy-start.32 = (f32[4096,2]{0,1:T(2,128)S(1)}, f32[4096,2]{0,1:T(2,128)}, u32[]{:S(2)}) copy-start(f32[4096,2]{0,1:T(2,128)} %copy-done.31) | copy-start | bytes 98308
  2336.0 15.6 all-to-all-start.9
  2339.3 286.4 %reduce-scatter.18.cloned.1.call-start = ((), (), s32[]{:S(2)}) async-start(), calls=%async_computation.29 | async-start | bytes 36864 | tf_op jit(solution)/shard_map/reduce_scatter | solution.py:291
  2339.3 12.3 copy-start.12
  2339.3 12.3 copy-start.42
  2353.0 273.4 %reduce-scatter.28.cloned.1.call-start = ((), (), s32[]{:S(2)}) async-start(), calls=%async_computation.34 | async-start | bytes 1769472
  2354.8 283.7 %reduce-scatter.20.cloned.1.call-start = ((), (), s32[]{:S(2)}) async-start(), calls=%async_computation.30 | async-start | bytes 4718592 | tf_op jit(solution)/shard_map/reduce_scatter | solution.py:294
  2362.1 293.0 %reduce-scatter.14.cloned.1.call-start = ((), (), s32[]{:S(2)}) async-start(), calls=%async_computation.27 | async-start | bytes 4718592 | tf_op jit(solution)/shard_map/reduce_scatter | solution.py:289
  2432.4 314.2 %reduce-scatter.12.cloned.1.call-start = ((), (), s32[]{:S(2)}) async-start(), calls=%async_computation.26 | async-start | bytes 4718592 | tf_op jit(solution)/shard_map/reduce_scatter | solution.py:288
  2502.1 336.0 %reduce-scatter.16.cloned.1.call-start = ((), (), s32[]{:S(2)}) async-start(), calls=%async_computation.28 | async-start | bytes 4718592 | tf_op jit(solution)/shard_map/reduce_scatter | solution.py:290
  2572.4 462.1 %reduce-scatter.22.cloned.1.call-start = ((), (), s32[]{:S(2)}) async-start(), calls=%async_computation.31 | async-start | bytes 12976128 | tf_op jit(solution)/shard_map/reduce_scatter | solution.py:296
  2584.6 645.5 %reduce-scatter.24.cloned.1.call-start = ((), (), s32[]{:S(2)}) async-start(), calls=%async_computation.32 | async-start | bytes 12976128 | tf_op jit(solution)/shard_map/reduce_scatter | solution.py:297
  2596.6 829.5 %reduce-scatter.26.cloned.1.call-start = ((), (), s32[]{:S(2)}) async-start(), calls=%async_computation.33 | async-start | bytes 12976128 | tf_op jit(solution)/shard_map/reduce_scatter | solution.py:298
  2608.6 891.6 %all-reduce.39.cloned.1.call-start = ((), (), s32[]{:S(2)}) async-start(), calls=%async_computation.35 | async-start | bytes 6422528 | tf_op jit(solution)/shard_map/psum | solution.py:302
  (56 other events, 233.8 us)
Sparse Core Ops, SparseCore 0:
  10.2 52.2 all-gather.11
  64.5 48.1 all-gather.13
  114.9 47.8 all-gather.9
  164.8 47.7 all-gather.15
  214.6 91.5 all-gather.17
  308.2 90.9 all-gather.19
  401.2 93.3 all-gather.21
  2353.1 52.4 reduce-scatter.17
  2409.0 63.8 reduce-scatter.27
  2476.9 86.8 reduce-scatter.19
  2567.4 87.6 reduce-scatter.13
  2659.0 87.6 reduce-scatter.11
  2750.3 87.7 reduce-scatter.15
  2842.0 192.4 reduce-scatter.21
  3038.3 191.7 reduce-scatter.23
  3234.0 192.0 reduce-scatter.25
  3430.2 69.9 all-reduce.38
where the time goes:
time: 3560 us; the launch traced here: 3520 us
  matrix products  1750 us (49%)
  waiting for transfers between devices  836 us (23%)
  local copies, waits for them, and re-layouts  408 us (11%)
  blocking collectives  241 us (7%)
  other arithmetic  195 us (5%)
  loops' own time  36.2 us (1%)
    dot_general x1280, matrix products, unit_inverse(): powered = jnp.einsum('gij,gjk->gik', powered, powered, precision=highest)  309 us
    dot_general x1280, matrix products, unit_inverse(): jnp.einsum('gij,gjk->gik', result, identity + powered, precision=highest)  295 us
    squeeze x320, local copies, waits for them, and re-layouts, recurrence(): lax.scan(jax.checkpoint(block_step), initial, (blocks(queries), blocks(ke...  224 us
    reduce_scatter x1, waiting for transfers between devices, local(): lax.psum_scatter(grad_gate_matrix, 'fsdp', scatter_dimension=0, tiled=True)  195 us
    reduce_scatter x1, waiting for transfers between devices, local(): lax.psum_scatter(grad_down, 'fsdp', scatter_dimension=1, tiled=True)  194 us
    reduce_scatter x1, waiting for transfers between devices, local(): lax.psum_scatter(grad_up_matrix, 'fsdp', scatter_dimension=0, tiled=True)  193 us
    dot_general x256, matrix products, block_step(): jnp.einsum('gij,gje->gie', inverse, values_rated, precision=highest)  166 us
    dot_general x256, matrix products, block_step(): jnp.einsum('gie,gje->gij', key_rows, key_rows)  137 us

commit v1 on v0

v1 whole, which is shorter than its diff:
```python
import functools

import jax
import jax.numpy as jnp
from jax import lax
from jax.experimental import pallas as pl
from jax.experimental.pallas import tpu as pltpu
from jax.sharding import PartitionSpec as P

CHUNK = 256
HALO = 16
TAPS = 4
MIB = 1024 * 1024

highest = lax.Precision.HIGHEST
epsilon = 1e-06
f32 = jnp.float32
bf16 = jnp.bfloat16


def nn(left_side, right_side):
    return lax.dot_general(
        left_side, right_side, (((1,), (0,)), ((), ())), preferred_element_type=f32
    )


def nt(left_side, right_side):
    return lax.dot_general(
        left_side, right_side, (((1,), (1,)), ((), ())), preferred_element_type=f32
    )


def tn(left_side, right_side):
    return lax.dot_general(
        left_side, right_side, (((0,), (0,)), ((), ())), preferred_element_type=f32
    )


def rms_scale(values, gain_vec):
    return (
        values * lax.rsqrt(jnp.mean(values * values, axis=-1, keepdims=True) + epsilon) * gain_vec
    )


def norm_backward(values, gain_vec, grad_out):
    scaling = lax.rsqrt(jnp.mean(values * values, axis=-1, keepdims=True) + epsilon)
    unit_rows = values * scaling
    gain_grad = jnp.sum(grad_out * unit_rows, axis=0)
    scaled_grad = grad_out * gain_vec
    input_grad = scaling * (
        scaled_grad - unit_rows * jnp.mean(scaled_grad * unit_rows, axis=-1, keepdims=True)
    )
    return (input_grad, gain_grad)


MESH = pl.DeviceIdType.MESH


class Place:
    def __init__(self, count):
        self.count = count
        self.sides = 2 if count % 2 == 0 else 1
        self.length = count // self.sides
        self.position = lax.axis_index("seq")
        self.index = lax.axis_index("fsdp")
        self.core = lax.rem(self.position, 2)
        self.side = lax.rem(self.index, self.sides)
        self.spot = lax.div(self.index, self.sides)

    def sibling(self):
        return {"seq": self.position + 1 - 2 * self.core, "fsdp": self.index}

    def across(self):
        return {"seq": lax.rem(self.position + 2, 4), "fsdp": self.index}

    def partner(self):
        return {"seq": self.position, "fsdp": self.spot * 2 + 1 - self.side}

    def ahead(self, step):
        spot = lax.rem(self.spot + step, self.length)
        return {"seq": self.position, "fsdp": spot * self.sides + self.side}

    def shard(self, spot, side):
        return spot * self.sides + side

    def behind(self, step):
        return lax.rem(self.spot + self.length - step, self.length)

    def greet(self, across):
        barrier = pltpu.get_barrier_semaphore()
        total = self.length

        def signal(device):
            pl.semaphore_signal(barrier, inc=1, device_id=device, device_id_type=MESH)

        def one(step, carry):
            signal(self.ahead(step))
            return carry

        lax.fori_loop(1, self.length, one, 0)
        signal(self.sibling())
        if self.sides == 2:
            signal(self.partner())
            total += 1
        if across:
            signal(self.across())
            total += 1
        pl.semaphore_wait(barrier, total)


def remote(source, target, send, recv, device):
    return pltpu.make_async_remote_copy(
        src_ref=source,
        dst_ref=target,
        send_sem=send,
        recv_sem=recv,
        device_id=device,
        device_id_type=MESH,
    )


def steps(first, last, body):
    def one(step, carry):
        body(step)
        return carry

    lax.fori_loop(first, last, one, 0)


class Gather:
    def __init__(self, count, shards, outs, sems):
        self.place = Place(count)
        self.shards, self.outs = shards, outs
        (
            self.line_send,
            self.line_recv,
            self.side_send,
            self.side_recv,
            self.core_send,
            self.core_recv,
            self.own,
        ) = sems

    @staticmethod
    def scratch(arrays, count):
        length = count // 2 if count % 2 == 0 else count
        return [
            pltpu.SemaphoreType.DMA((arrays, length)),
            pltpu.SemaphoreType.DMA((arrays, length)),
            pltpu.SemaphoreType.DMA((arrays, length)),
            pltpu.SemaphoreType.DMA((arrays, length)),
            pltpu.SemaphoreType.DMA((arrays, 2 * length)),
            pltpu.SemaphoreType.DMA((arrays, 2 * length)),
            pltpu.SemaphoreType.DMA((arrays,)),
        ]

    def half(self, a, core):
        width = self.shards[a].shape[1] // 2
        return pl.ds(pl.multiple_of(core * width, 128), width)

    def spot(self, a, shard, core):
        depth = self.shards[a].shape[0]
        return self.outs[a].at[
            pl.ds(pl.multiple_of(shard * depth, depth), depth), self.half(a, core)
        ]

    def line(self, a, step, arriving):
        p = self.place
        shard = p.shard(p.behind(step), p.side) if arriving else p.index
        target = self.spot(a, shard, p.core)
        source = target if arriving else self.shards[a].at[:, self.half(a, p.core)]
        return remote(
            source, target, self.line_send.at[a, step], self.line_recv.at[a, step], p.ahead(step)
        )

    def side(self, a, step, arriving):
        p = self.place
        shard = p.shard(p.behind(step), 1 - p.side if arriving else p.side)
        target = self.spot(a, shard, p.core)
        return remote(
            target, target, self.side_send.at[a, step], self.side_recv.at[a, step], p.partner()
        )

    def side_own(self, a):
        p = self.place
        return remote(
            self.shards[a].at[:, self.half(a, p.core)],
            self.spot(a, p.index, p.core),
            self.side_send.at[a, 0],
            self.side_recv.at[a, 0],
            p.partner(),
        )

    def core(self, a, step, other, arriving):
        p = self.place
        shard = p.shard(p.behind(step), 1 - p.side if other else p.side)
        target = self.spot(a, shard, 1 - p.core if arriving else p.core)
        slot = 2 * step + (1 if other else 0)
        return remote(
            target, target, self.core_send.at[a, slot], self.core_recv.at[a, slot], p.sibling()
        )

    def keep(self, a):
        depth = self.shards[a].shape[0]
        rows = pl.ds(pl.multiple_of(self.place.index * depth, depth), depth)
        return pltpu.make_async_copy(self.shards[a], self.outs[a].at[rows, :], self.own.at[a])

    def start(self, a):
        if self.place.sides == 2:
            self.side_own(a).start()
        steps(1, self.place.length, lambda step: self.line(a, step, False).start())
        self.keep(a).start()

    def forward(self, a):
        def one(step):
            self.line(a, step, True).wait_recv()
            if self.place.sides == 2:
                self.side(a, step, False).start()
            self.core(a, step, False, False).start()

        steps(1, self.place.length, one)

    def spread(self, a):
        def one(step):
            self.side(a, step, True).wait_recv()
            self.core(a, step, True, False).start()

        if self.place.sides == 2:
            steps(0, self.place.length, one)

    def finish(self, a):
        p = self.place
        self.keep(a).wait()

        def own(step):
            self.line(a, step, False).wait_send()
            self.core(a, step, False, False).wait_send()
            self.core(a, step, False, True).wait_recv()

        steps(1, p.length, own)
        if p.sides == 2:
            self.side_own(a).wait_send()
            steps(1, p.length, lambda step: self.side(a, step, False).wait_send())

            def other(step):
                self.core(a, step, True, False).wait_send()
                self.core(a, step, True, True).wait_recv()

            steps(0, p.length, other)


def gather_kernel(arrays, count, *refs):
    gather = Gather(count, refs[:arrays], refs[arrays : 2 * arrays], refs[2 * arrays :])
    gather.place.greet(False)
    for a in range(arrays):
        gather.start(a)
    for a in range(arrays + 1):
        if a < arrays:
            gather.forward(a)
        if a > 0:
            gather.spread(a - 1)
    for a in range(arrays):
        gather.finish(a)


def gather_all(shards, collective_id):
    count = lax.axis_size("fsdp")
    arrays = len(shards)
    anywhere = pl.BlockSpec(memory_space=pl.ANY)
    return pl.pallas_call(
        functools.partial(gather_kernel, arrays, count),
        in_specs=[anywhere] * arrays,
        out_specs=[anywhere] * arrays,
        out_shape=[
            jax.ShapeDtypeStruct((count * s.shape[0], s.shape[1]), s.dtype) for s in shards
        ],
        scratch_shapes=Gather.scratch(arrays, count),
        compiler_params=pltpu.CompilerParams(collective_id=collective_id, has_side_effects=True),
    )(*shards)


class Reduce:
    def __init__(self, count, pieces, sources, outs, buffers, sems):
        self.place = Place(count)
        self.pieces, self.sources, self.outs = pieces, sources, outs
        self.total, self.core_in, self.side_in, self.line_in, self.across_in, self.done = buffers
        (
            self.core_sem,
            self.load_sem,
            self.side_sem,
            self.line_sem,
            self.across_sem,
            self.last_sem,
            self.store_sem,
        ) = sems

    @staticmethod
    def plan(widths, limit):
        pieces = []
        for a, width in enumerate(widths):
            tiles = width // 256
            parts = -(-tiles * 128 // limit)
            offset = 0
            for part in range(parts):
                wide = (tiles // parts + (1 if part < tiles % parts else 0)) * 128
                pieces.append((a, offset, wide))
                offset += wide
        return pieces

    @staticmethod
    def scratch(count, pieces, depths):
        sides = 2 if count % 2 == 0 else 1
        length = count // sides
        pairs = [(depths[a], wide) for a, _, wide in pieces]
        number = len(pieces)

        def stack(lead):
            return [pltpu.VMEM(lead + pair, bf16) for pair in pairs]

        shapes = (
            stack((count,)) + stack((count,)) + stack((length,)) + stack((length,))
            + stack(()) + stack(())
        )
        sems = [
            pltpu.SemaphoreType.DMA((number, 2)),
            pltpu.SemaphoreType.DMA((number,)),
            pltpu.SemaphoreType.DMA((number, 2, length)),
            pltpu.SemaphoreType.DMA((number, 2, length)),
            pltpu.SemaphoreType.DMA((number, 2)),
            pltpu.SemaphoreType.DMA((number, 2)),
            pltpu.SemaphoreType.DMA((number,)),
        ]
        return shapes + sems

    @staticmethod
    def split(refs, number):
        buffers = [refs[i * number : (i + 1) * number] for i in range(6)]
        return buffers, refs[6 * number :]

    def columns(self, p, core):
        a, offset, wide = self.pieces[p]
        width = self.sources[a].shape[2] // 2
        return a, pl.ds(pl.multiple_of(core * width + offset, 128), wide)

    def to_sibling(self, p):
        a, columns = self.columns(p, 1 - self.place.core)
        return remote(
            self.sources[a].at[:, :, columns],
            self.core_in[p],
            self.core_sem.at[p, 0],
            self.core_sem.at[p, 1],
            self.place.sibling(),
        )

    def load(self, p):
        a, columns = self.columns(p, self.place.core)
        return pltpu.make_async_copy(
            self.sources[a].at[:, :, columns], self.total[p], self.load_sem.at[p]
        )

    def to_side(self, p, spot):
        place = self.place
        return remote(
            self.total[p].at[place.shard(spot, 1 - place.side)],
            self.side_in[p].at[spot],
            self.side_sem.at[p, 0, spot],
            self.side_sem.at[p, 1, spot],
            place.partner(),
        )

    def to_line(self, p, step):
        place = self.place
        spot = lax.rem(place.spot + step, place.length)
        return remote(
            self.total[p].at[place.shard(spot, place.side)],
            self.line_in[p].at[step],
            self.line_sem.at[p, 0, step],
            self.line_sem.at[p, 1, step],
            place.ahead(step),
        )

    def to_across(self, p):
        return remote(
            self.done[p],
            self.across_in[p],
            self.across_sem.at[p, 0],
            self.across_sem.at[p, 1],
            self.place.across(),
        )

    def target(self, p, core):
        a, columns = self.columns(p, core)
        return self.outs[a].at[:, columns]

    def to_result(self, p, arriving):
        core = 1 - self.place.core if arriving else self.place.core
        return remote(
            self.across_in[p],
            self.target(p, core),
            self.last_sem.at[p, 0],
            self.last_sem.at[p, 1],
            self.place.sibling(),
        )

    def store(self, p):
        return pltpu.make_async_copy(
            self.across_in[p], self.target(p, self.place.core), self.store_sem.at[p]
        )

    def start(self, p):
        self.to_sibling(p).start()
        self.load(p).start()

    def stage_core(self, p):
        place = self.place
        self.load(p).wait()
        self.to_sibling(p).wait_recv()
        if place.sides == 2:

            def one(step):
                spot = lax.rem(place.spot + step, place.length)
                shard = place.shard(spot, 1 - place.side)
                self.total[p][shard] = (
                    self.total[p][shard].astype(f32) + self.core_in[p][shard].astype(f32)
                ).astype(bf16)
                self.to_side(p, spot).start()

            steps(1, place.length + 1, one)

    def stage_side(self, p):
        place = self.place

        def one(step):
            spot = lax.rem(place.spot + step, place.length)
            shard = place.shard(spot, place.side)
            total = self.total[p][shard].astype(f32) + self.core_in[p][shard].astype(f32)
            if place.sides == 2:
                self.to_side(p, spot).wait_recv()
                total = total + self.side_in[p][spot].astype(f32)
            self.total[p][shard] = total.astype(bf16)

        def send(step):
            one(step)
            self.to_line(p, step).start()

        steps(1, place.length, send)
        one(0)

    def stage_line(self, p):
        place = self.place
        self.done[p][...] = self.total[p][place.index]

        def one(step):
            self.to_line(p, step).wait_recv()

        steps(1, place.length, one)
        total = self.total[p][place.index].astype(f32)
        if place.length <= 8:
            for step in range(1, place.length):
                total = total + self.line_in[p][step].astype(f32)
        else:
            total = lax.fori_loop(
                1,
                place.length,
                lambda step, carry: carry + self.line_in[p][step].astype(f32),
                total,
            )
        self.done[p][...] = total.astype(bf16)
        self.to_across(p).start()

    def stage_across(self, p):
        copy = self.to_across(p)
        copy.wait_recv()
        self.across_in[p][...] = (
            self.across_in[p][...].astype(f32) + self.done[p][...].astype(f32)
        ).astype(bf16)
        self.to_result(p, False).start()
        self.store(p).start()

    def finish(self, p):
        place = self.place
        self.to_sibling(p).wait_send()
        if place.sides == 2:
            steps(0, place.length, lambda spot: self.to_side(p, spot).wait_send())
        steps(1, place.length, lambda step: self.to_line(p, step).wait_send())
        self.to_across(p).wait_send()
        self.to_result(p, False).wait_send()
        self.to_result(p, True).wait_recv()
        self.store(p).wait()


def reduce_kernel(arrays, count, pieces, *refs):
    buffers, sems = Reduce.split(refs[2 * arrays :], len(pieces))
    reduce = Reduce(count, pieces, refs[:arrays], refs[arrays : 2 * arrays], buffers, sems)
    reduce.place.greet(True)
    number = len(pieces)
    for p in range(number):
        reduce.start(p)
    stages = (reduce.stage_core, reduce.stage_side, reduce.stage_line, reduce.stage_across)
    for turn in range(number + len(stages) - 1):
        for behind, stage in enumerate(stages):
            if 0 <= turn - behind < number:
                stage(turn - behind)
    for p in range(number):
        reduce.finish(p)


def reduce_all(sources, collective_id, limit=768):
    count = lax.axis_size("fsdp")
    arrays = len(sources)
    views = [s.reshape(count, s.shape[0] // count, s.shape[1]) for s in sources]
    pieces = Reduce.plan([s.shape[1] for s in sources], limit)
    anywhere = pl.BlockSpec(memory_space=pl.ANY)
    return pl.pallas_call(
        functools.partial(reduce_kernel, arrays, count, pieces),
        in_specs=[anywhere] * arrays,
        out_specs=[anywhere] * arrays,
        out_shape=[jax.ShapeDtypeStruct(v.shape[1:], bf16) for v in views],
        scratch_shapes=Reduce.scratch(count, pieces, [v.shape[1] for v in views]),
        compiler_params=pltpu.CompilerParams(
            collective_id=collective_id, has_side_effects=True, vmem_limit_bytes=60 * MIB
        ),
    )(*views)


PACK = (16, 256)


def pack_shard(parts):
    flat = jnp.concatenate([part.reshape(-1).astype(bf16) for part in parts])
    return jnp.pad(flat, (0, PACK[0] * PACK[1] - flat.shape[0])).reshape(PACK)


def pack_shards(parts):
    count = parts[0].shape[0]
    flat = jnp.concatenate([part.reshape(count, -1).astype(bf16) for part in parts], axis=1)
    flat = jnp.pad(flat, ((0, 0), (0, PACK[0] * PACK[1] - flat.shape[1])))
    return flat.reshape(count * PACK[0], PACK[1])


def unpack(flat, shapes):
    parts, offset = [], 0
    for shape in shapes:
        size = 1
        for extent in shape:
            size *= extent
        parts.append(flat[:, offset : offset + size].reshape((flat.shape[0],) + tuple(shape)))
        offset += size
    return parts


def grid_indices():
    row = lax.broadcasted_iota(jnp.int32, (CHUNK, CHUNK), 0)
    col = lax.broadcasted_iota(jnp.int32, (CHUNK, CHUNK), 1)
    return row, col


def conv_pre(wide_ref, taps, rows):
    total = None
    for offset in range(TAPS):
        term = taps[offset : offset + 1, :] * wide_ref[pl.ds(HALO - TAPS + 1 + offset, rows), :]
        total = term if total is None else total + term
    return total


def sigmoid(values):
    return 1.0 / (1.0 + jnp.exp(-values))


def head_column(table, head):
    lane = lax.broadcasted_iota(jnp.int32, table.shape, 1)
    return jnp.sum(jnp.where(lane == head, table, 0.0), axis=1, keepdims=True)


def forward_kernel(
    q_ref,
    k_ref,
    v_ref,
    logit_ref,
    taps_ref,
    out_ref,
    carry_ref,
    fresh_ref,
    inverse_ref,
    starts_ref,
    final_ref,
    wide,
    level_masks,
):
    head = pl.program_id(0)
    rows = out_ref.shape[0]
    size = out_ref.shape[1]
    chunks = rows // CHUNK
    levels = CHUNK.bit_length() - 1
    row, col = grid_indices()

    @pl.when(head == 0)
    def _():
        for level in range(levels):
            same = (row >> (level + 1)) == (col >> (level + 1))
            below = ((row >> level) & 1 == 1) & ((col >> level) & 1 == 0)
            level_masks[level] = jnp.where(same & below, 1.0, 0.0).astype(bf16)

    lows = []
    for which, ref in enumerate((q_ref, k_ref, v_ref)):
        wide[...] = ref[...].astype(f32)
        pre = conv_pre(wide, taps_ref[0, which].astype(f32), rows)
        act = pre * sigmoid(pre)
        if which < 2:
            act = act * lax.rsqrt(jnp.sum(act * act, axis=1, keepdims=True) + epsilon)
        lows.append(act.astype(bf16))
    queries, keys, values = lows
    rates = sigmoid(head_column(logit_ref[...].astype(f32), head))
    scaling = size ** (-0.5)
    eye = jnp.where(row == col, 1.0, 0.0)
    lower = row >= col

    parts = [slice(chunk * CHUNK, (chunk + 1) * CHUNK) for chunk in range(chunks)]
    stricts = [(rates[p] * nt(keys[p], keys[p])).astype(bf16) for p in parts]
    results = [eye - (strict * level_masks[0]).astype(f32) for strict in stricts]
    scores = [jnp.where(lower, nt(queries[p], keys[p]), 0.0).astype(bf16) for p in parts]
    for level in range(1, levels):
        mask = level_masks[level]
        lows = [result.astype(bf16) for result in results]
        inners = [nn(low, strict * mask).astype(bf16) for low, strict in zip(lows, stricts)]
        results = [
            result - nn(inner, low) for result, inner, low in zip(results, inners, lows)
        ]
    inverses = [result.astype(bf16) for result in results]
    for part, inverse in zip(parts, inverses):
        inverse_ref[part, :] = inverse

    srow = lax.broadcasted_iota(jnp.int32, (size, size), 0)
    scol = lax.broadcasted_iota(jnp.int32, (size, size), 1)
    memory = jnp.concatenate(
        [jnp.zeros((size, size), f32), jnp.where(srow == scol, 1.0, 0.0)], axis=1
    )
    for chunk in range(chunks):
        part = slice(chunk * CHUNK, (chunk + 1) * CHUNK)
        key_part, query_part, rate_part = keys[part], queries[part], rates[part]
        low_memory = memory.astype(bf16)
        starts_ref[0, chunk] = low_memory
        seen = nn(key_part, low_memory)
        aim = jnp.concatenate([values[part].astype(f32), jnp.zeros((CHUNK, size), f32)], axis=1)
        aim = (rate_part * (aim - seen)).astype(bf16)
        fresh = nn(inverses[chunk], aim).astype(bf16)
        fresh_ref[part, :] = fresh
        both = scaling * (nn(query_part, low_memory) + nn(scores[chunk], fresh))
        out_ref[part, :] = both[:, :size]
        carry_ref[part, :] = both[:, size:].astype(bf16)
        memory = memory + tn(key_part, fresh)
    final_ref[0] = memory


def delta_forward(queries, keys, values, logits, taps):
    wide_rows, width = queries.shape
    heads = logits.shape[1]
    size = width // heads
    rows = wide_rows - HALO
    chunks = rows // CHUNK
    column = pl.BlockSpec((wide_rows, size), lambda h: (0, h))
    plain = pl.BlockSpec((rows, size), lambda h: (0, h))
    return pl.pallas_call(
        forward_kernel,
        grid=(heads,),
        in_specs=[
            column,
            column,
            column,
            pl.BlockSpec((rows, heads), lambda h: (0, 0)),
            pl.BlockSpec((1, 3, TAPS, size), lambda h: (h, 0, 0, 0)),
        ],
        out_specs=[
            plain,
            plain,
            pl.BlockSpec((rows, 2 * size), lambda h: (0, h)),
            pl.BlockSpec((rows, CHUNK), lambda h: (0, h)),
            pl.BlockSpec((1, chunks, size, 2 * size), lambda h: (h, 0, 0, 0)),
            pl.BlockSpec((1, size, 2 * size), lambda h: (h, 0, 0)),
        ],
        out_shape=[
            jax.ShapeDtypeStruct((rows, width), f32),
            jax.ShapeDtypeStruct((rows, width), bf16),
            jax.ShapeDtypeStruct((rows, 2 * width), bf16),
            jax.ShapeDtypeStruct((rows, heads * CHUNK), bf16),
            jax.ShapeDtypeStruct((heads, chunks, size, 2 * size), bf16),
            jax.ShapeDtypeStruct((heads, size, 2 * size), f32),
        ],
        scratch_shapes=[
            pltpu.VMEM((wide_rows, size), f32),
            pltpu.VMEM((CHUNK.bit_length() - 1, CHUNK, CHUNK), bf16),
        ],
        compiler_params=pltpu.CompilerParams(vmem_limit_bytes=48 * MIB),
    )(queries, keys, values, logits, taps)


def mix_kernel(out_ref, carry_ref, state_ref, gain_ref, mixed_ref):
    output = out_ref[...] + nn(carry_ref[...], state_ref[0].astype(bf16))
    gain = gain_ref[...].astype(f32)
    mixed_ref[...] = rms_scale(output, gain).astype(bf16)


def mix(outputs, carries, states, gain):
    rows, width = outputs.shape
    heads, size, _ = states.shape
    plain = pl.BlockSpec((rows, size), lambda h: (0, h))
    return pl.pallas_call(
        mix_kernel,
        grid=(heads,),
        in_specs=[
            plain,
            plain,
            pl.BlockSpec((1, size, size), lambda h: (h, 0, 0)),
            pl.BlockSpec((1, size), lambda h: (0, 0)),
        ],
        out_specs=plain,
        out_shape=jax.ShapeDtypeStruct((rows, width), bf16),
        compiler_params=pltpu.CompilerParams(vmem_limit_bytes=32 * MIB),
    )(outputs, carries, states, gain)


def unmix_kernel(
    out_ref, carry_ref, state_ref, gain_ref, grad_ref, grad_out_ref, grad_state_ref, grad_gain_ref
):
    output = out_ref[...] + nn(carry_ref[...], state_ref[0].astype(bf16))
    gain = gain_ref[...].astype(f32)
    grad = grad_ref[...].astype(f32)
    scaling = lax.rsqrt(jnp.mean(output * output, axis=1, keepdims=True) + epsilon)
    unit_rows = output * scaling

    @pl.when(pl.program_id(0) == 0)
    def _():
        grad_gain_ref[...] = jnp.zeros_like(grad_gain_ref)

    grad_gain_ref[...] += jnp.sum(grad * unit_rows, axis=0, keepdims=True)
    scaled = grad * gain
    grad_out = scaling * (scaled - unit_rows * jnp.mean(scaled * unit_rows, axis=1, keepdims=True))
    low_grad = grad_out.astype(bf16)
    grad_state_ref[0] = tn(carry_ref[...], low_grad)
    grad_out_ref[...] = (grad_out * output.shape[1] ** (-0.5)).astype(bf16)


def unmix(outputs, carries, states, gain, grad_heads):
    rows, width = outputs.shape
    heads, size, _ = states.shape
    plain = pl.BlockSpec((rows, size), lambda h: (0, h))
    state = pl.BlockSpec((1, size, size), lambda h: (h, 0, 0))
    vector = pl.BlockSpec((1, size), lambda h: (0, 0))
    return pl.pallas_call(
        unmix_kernel,
        grid=(heads,),
        in_specs=[plain, plain, state, vector, plain],
        out_specs=[plain, state, vector],
        out_shape=[
            jax.ShapeDtypeStruct((rows, width), bf16),
            jax.ShapeDtypeStruct((heads, size, size), f32),
            jax.ShapeDtypeStruct((1, size), f32),
        ],
        compiler_params=pltpu.CompilerParams(vmem_limit_bytes=32 * MIB),
    )(outputs, carries, states, gain, grad_heads)


def backward_kernel(
    q_ref,
    k_ref,
    v_ref,
    logit_ref,
    taps_ref,
    grad_ref,
    fresh_ref,
    inverse_ref,
    starts_ref,
    state_ref,
    grad_state_ref,
    grad_q_ref,
    grad_k_ref,
    grad_v_ref,
    tails_ref,
    heads_ref,
    grad_taps_ref,
    grad_logit_ref,
    wides,
    pres,
    grads,
    padded,
):
    head = pl.program_id(0)
    rows, size = grad_ref.shape
    chunks = rows // CHUNK
    row, col = grid_indices()
    lower, upper = row >= col, row <= col

    lows, scales = [], []
    for which, ref in enumerate((q_ref, k_ref, v_ref)):
        wides[which] = ref[...].astype(f32)
        pre = conv_pre(wides.at[which], taps_ref[0, which].astype(f32), rows)
        pres[which] = pre
        act = pre * sigmoid(pre)
        if which < 2:
            scale = lax.rsqrt(jnp.sum(act * act, axis=1, keepdims=True) + epsilon)
            act = act * scale
            scales.append(scale)
        lows.append(act.astype(bf16))
    queries, keys, values = lows
    rates = sigmoid(head_column(logit_ref[...].astype(f32), head))

    state_in = state_ref[0].astype(bf16)
    pairs = fresh_ref[...]
    fresh_all = (pairs[:, :size].astype(f32) + nn(pairs[:, size:], state_in)).astype(bf16)

    grad_memory = grad_state_ref[0]
    grad_rates = [None] * chunks
    for chunk in reversed(range(chunks)):
        part = slice(chunk * CHUNK, (chunk + 1) * CHUNK)
        key, query, rate = keys[part], queries[part], rates[part]
        value = values[part]
        grad_out = grad_ref[part, :]
        fresh = fresh_all[part]
        start = starts_ref[0, chunk]
        memory = (start[:, :size].astype(f32) + nn(start[:, size:], state_in)).astype(bf16)
        low_grad = grad_memory.astype(bf16)
        key_f = key.astype(f32)
        rated = (rate * key_f).astype(bf16)

        scores_t = jnp.where(upper, nt(key, query), 0.0).astype(bf16)
        grad_fresh = (nn(scores_t, grad_out) + nn(key, low_grad)).astype(bf16)
        aim = tn(inverse_ref[part, :], grad_fresh)
        low_aim = aim.astype(bf16)
        grad_memory = grad_memory + tn(query, grad_out) - tn(rated, low_aim)

        grad_scores = jnp.where(lower, nt(grad_out, fresh), 0.0).astype(bf16)
        grad_scores_t = jnp.where(upper, nt(fresh, grad_out), 0.0).astype(bf16)
        grad_strict = jnp.where(row > col, nt(low_aim, fresh), 0.0).astype(bf16)
        grad_strict_t = jnp.where(row < col, nt(fresh, low_aim), 0.0).astype(bf16)

        grad_query = nt(grad_out, memory) + nn(grad_scores, key)
        inner = -(nn(grad_strict, key) + nt(low_aim, memory))
        grad_rates[chunk] = jnp.sum(key_f * inner + value.astype(f32) * aim, axis=1, keepdims=True)
        grad_key = (
            rate * inner
            - nn(grad_strict_t, rated)
            + nn(grad_scores_t, query)
            + nt(fresh, low_grad)
        )
        grads[0, part, :] = grad_query
        grads[1, part, :] = grad_key
        grads[2, part, :] = rate * aim

    grad_rate = jnp.concatenate(grad_rates, axis=0)
    grad_logit = grad_rate * rates * (1.0 - rates)
    lane = lax.broadcasted_iota(jnp.int32, grad_logit_ref.shape, 1)

    @pl.when(head == 0)
    def _():
        grad_logit_ref[...] = jnp.zeros_like(grad_logit_ref)
        padded[...] = jnp.zeros_like(padded)

    grad_logit_ref[...] = jnp.where(lane == head, grad_logit, grad_logit_ref[...])

    for which, ref in enumerate((grad_q_ref, grad_k_ref, grad_v_ref)):
        taps = taps_ref[0, which].astype(f32)
        pre = pres[which]
        sig = sigmoid(pre)
        grad_act = grads[which]
        if which < 2:
            scale = scales[which]
            unit_rows = pre * sig * scale
            grad_act = scale * (
                grad_act - unit_rows * jnp.sum(grad_act * unit_rows, axis=1, keepdims=True)
            )
        grad_pre = grad_act * sig * (1.0 + pre * (1.0 - sig))
        padded[pl.ds(HALO, rows), :] = grad_pre
        for offset in range(TAPS):
            shifted = wides[which, pl.ds(HALO - TAPS + 1 + offset, rows), :]
            grad_taps_ref[0, which, pl.ds(offset, 1), :] = jnp.sum(
                grad_pre * shifted, axis=0, keepdims=True
            )

        def back(start, count):
            total = None
            for offset in range(TAPS):
                term = (
                    taps[offset : offset + 1, :]
                    * padded[pl.ds(start + TAPS - 1 - offset, count), :]
                )
                total = term if total is None else total + term
            return total

        grad_signal = back(HALO, rows)
        ref[...] = grad_signal.astype(bf16)
        tails_ref[0, which] = grad_signal[rows - HALO :]
        heads_ref[0, which] = back(0, HALO)


def delta_backward(
    queries, keys, values, logits, taps, grad_out, fresh, inverses, starts, state, grad_state
):
    wide_rows, width = queries.shape
    heads = logits.shape[1]
    size = width // heads
    rows = wide_rows - HALO
    chunks = rows // CHUNK
    column = pl.BlockSpec((wide_rows, size), lambda h: (0, h))
    plain = pl.BlockSpec((rows, size), lambda h: (0, h))
    whole = pl.BlockSpec((rows, heads), lambda h: (0, 0))
    tap = pl.BlockSpec((1, 3, TAPS, size), lambda h: (h, 0, 0, 0))
    state_spec = pl.BlockSpec((1, size, size), lambda h: (h, 0, 0))
    edge = pl.BlockSpec((1, 3, HALO, size), lambda h: (h, 0, 0, 0))
    return pl.pallas_call(
        backward_kernel,
        grid=(heads,),
        in_specs=[
            column,
            column,
            column,
            whole,
            tap,
            plain,
            pl.BlockSpec((rows, 2 * size), lambda h: (0, h)),
            pl.BlockSpec((rows, CHUNK), lambda h: (0, h)),
            pl.BlockSpec((1, chunks, size, 2 * size), lambda h: (h, 0, 0, 0)),
            state_spec,
            state_spec,
        ],
        out_specs=[plain, plain, plain, edge, edge, tap, whole],
        out_shape=[
            jax.ShapeDtypeStruct((rows, width), bf16),
            jax.ShapeDtypeStruct((rows, width), bf16),
            jax.ShapeDtypeStruct((rows, width), bf16),
            jax.ShapeDtypeStruct((heads, 3, HALO, size), f32),
            jax.ShapeDtypeStruct((heads, 3, HALO, size), f32),
            jax.ShapeDtypeStruct((heads, 3, TAPS, size), f32),
            jax.ShapeDtypeStruct((rows, heads), f32),
        ],
        scratch_shapes=[
            pltpu.VMEM((3, wide_rows, size), f32),
            pltpu.VMEM((3, rows, size), f32),
            pltpu.VMEM((3, rows, size), f32),
            pltpu.VMEM((rows + 2 * HALO, size), f32),
        ],
        compiler_params=pltpu.CompilerParams(vmem_limit_bytes=56 * MIB),
    )(
        queries,
        keys,
        values,
        logits,
        taps,
        grad_out,
        fresh,
        inverses,
        starts,
        state,
        grad_state,
    )


def batched(left_side, right_side, transpose_left=False):
    return lax.dot_general(
        left_side,
        right_side,
        (((1 if transpose_left else 2,), (1,)), ((0,), (0,))),
        precision=highest,
        preferred_element_type=f32,
    )


def local(
    inputs,
    g_attn,
    w_query,
    w_key,
    w_value,
    w_beta,
    conv_taps,
    o_gain,
    w_out,
    g_mlp,
    w_gate,
    w_up,
    w_down,
    cotangent,
):
    count = lax.axis_size("fsdp")
    small = (g_attn.shape, g_mlp.shape, o_gain.shape, conv_taps.shape, w_beta.shape)
    packed = pack_shard((g_attn, g_mlp, o_gain, conv_taps, w_beta))
    packed, w_query, w_key, w_value, w_out = gather_all(
        (packed, w_query, w_key, w_value, w_out), 0
    )
    w_gate, w_up, w_down_t = gather_all((w_gate, w_up, jnp.transpose(w_down)), 1)
    g_attn, g_mlp, o_gain, conv_taps, w_beta = unpack(packed.reshape(count, -1), small)
    g_attn, g_mlp, o_gain = g_attn.reshape(-1), g_mlp.reshape(-1), o_gain.reshape(-1)
    conv_taps = jnp.transpose(conv_taps, (1, 0, 2)).reshape(conv_taps.shape[1], -1)
    w_beta = w_beta.reshape(-1, w_beta.shape[2])

    groups = lax.axis_size("seq")
    position = lax.axis_index("seq")
    forward_pairs = [(index, index + 1) for index in range(groups - 1)]
    backward_pairs = [(index + 1, index) for index in range(groups - 1)]
    tokens_low = inputs[0]
    rows, width = tokens_low.shape
    heads = w_beta.shape[1]
    size = o_gain.shape[0]
    halo = lax.ppermute(tokens_low[rows - HALO :], "seq", forward_pairs)
    gain_attn = g_attn.astype(f32)
    wide_tokens = jnp.concatenate([halo, tokens_low], axis=0).astype(f32)
    tokens = tokens_low.astype(f32)
    wide_normed = rms_scale(wide_tokens, gain_attn).astype(bf16)
    normed = wide_normed[HALO:]

    queries = nn(wide_normed, w_query).astype(bf16)
    keys = nn(wide_normed, w_key).astype(bf16)
    values = nn(wide_normed, w_value).astype(bf16)
    logits = nn(normed, w_beta).astype(bf16)
    taps = jnp.transpose(conv_taps.reshape(TAPS, 3, heads, size), (2, 1, 0, 3))

    outputs, carries, fresh, inverses, starts, finals = delta_forward(
        queries, keys, values, logits, taps
    )

    finals_all = lax.all_gather(finals, "seq", axis=0)
    state = jnp.zeros((heads, size, size), f32)
    states = [state]
    for index in range(groups - 1):
        state = finals_all[index, :, :, :size] + batched(finals_all[index, :, :, size:], state)
        states.append(state)
    state_in = lax.dynamic_index_in_dim(jnp.stack(states), position, 0, keepdims=False)

    gain_out = o_gain.reshape(1, size)
    head_rows = mix(outputs, carries, state_in, gain_out)
    attended = tokens + nn(head_rows, w_out)
    gain_mlp = g_mlp.astype(f32)
    normed_ff = rms_scale(attended, gain_mlp).astype(bf16)
    gated = nn(normed_ff, w_gate)
    upward = nn(normed_ff, w_up)
    sigmoid_gate = jax.nn.sigmoid(gated)
    activated = gated * sigmoid_gate
    hidden = (activated * upward).astype(bf16)
    layer_out = (attended + nt(hidden, w_down_t)).astype(bf16)

    grad_out = cotangent[0]
    grad_down_t = tn(grad_out, hidden).astype(bf16)
    grad_hidden = nn(grad_out, w_down_t)
    grad_gate = (grad_hidden * upward * sigmoid_gate * (1.0 + gated * (1.0 - sigmoid_gate))).astype(
        bf16
    )
    grad_upward = (grad_hidden * activated).astype(bf16)
    grad_gate_matrix = tn(normed_ff, grad_gate).astype(bf16)
    grad_up_matrix = tn(normed_ff, grad_upward).astype(bf16)
    grad_normed_ff = nt(grad_gate, w_gate) + nt(grad_upward, w_up)
    grad_from_ff, grad_gain_mlp = norm_backward(attended, gain_mlp, grad_normed_ff)
    grad_attended = grad_out.astype(f32) + grad_from_ff

    grad_mixed = grad_attended.astype(bf16)
    grad_out_matrix = tn(head_rows, grad_mixed).astype(bf16)
    grad_heads = nt(grad_mixed, w_out).astype(bf16)
    grad_delta, grad_starts, grad_gain_out = unmix(
        outputs, carries, state_in, gain_out, grad_heads
    )
    grads_all = lax.all_gather(grad_starts, "seq", axis=0)
    grad_state = jnp.zeros((heads, size, size), f32)
    grad_states = [grad_state]
    for index in reversed(range(1, groups)):
        grad_state = grads_all[index] + batched(
            finals_all[index, :, :, size:], grad_state, transpose_left=True
        )
        grad_states.append(grad_state)
    grad_states.reverse()
    grad_final = lax.dynamic_index_in_dim(jnp.stack(grad_states), position, 0, keepdims=False)

    grad_q, grad_k, grad_v, tails, firsts, grad_taps, grad_logits = delta_backward(
        queries,
        keys,
        values,
        logits,
        taps,
        grad_delta,
        fresh,
        inverses,
        starts,
        state_in,
        grad_final,
    )
    received = lax.ppermute(firsts, "seq", backward_pairs)
    fixed = jnp.transpose((tails + received).astype(bf16), (1, 2, 0, 3)).reshape(3, HALO, width)
    grad_q = lax.dynamic_update_slice(grad_q, fixed[0], (rows - HALO, 0))
    grad_k = lax.dynamic_update_slice(grad_k, fixed[1], (rows - HALO, 0))
    grad_v = lax.dynamic_update_slice(grad_v, fixed[2], (rows - HALO, 0))
    grad_logits = grad_logits.astype(bf16)

    grad_query_matrix = tn(normed, grad_q).astype(bf16)
    grad_key_matrix = tn(normed, grad_k).astype(bf16)
    grad_value_matrix = tn(normed, grad_v).astype(bf16)
    grad_beta_matrix = tn(normed, grad_logits)
    grad_normed = (
        nt(grad_q, w_query) + nt(grad_k, w_key) + nt(grad_v, w_value) + nt(grad_logits, w_beta)
    )
    grad_from_attn, grad_gain_attn = norm_backward(tokens, gain_attn, grad_normed)
    grad_inputs = (grad_attended + grad_from_attn)[None]
    grad_taps = jnp.transpose(grad_taps, (2, 1, 0, 3)).reshape(TAPS, count, -1)
    packed = pack_shards(
        (
            grad_gain_attn.reshape(count, -1),
            grad_gain_mlp.reshape(count, -1),
            grad_gain_out.reshape(count, -1),
            jnp.transpose(grad_taps, (1, 0, 2)),
            grad_beta_matrix.reshape(count, -1),
        )
    )
    grad_gate_matrix, grad_up_matrix, grad_down_t = reduce_all(
        (grad_gate_matrix, grad_up_matrix, grad_down_t), 2
    )
    packed, grad_query_matrix, grad_key_matrix, grad_value_matrix, grad_out_matrix = reduce_all(
        (packed, grad_query_matrix, grad_key_matrix, grad_value_matrix, grad_out_matrix), 3
    )
    parts = [part[0].astype(f32) for part in unpack(packed.reshape(1, -1), small)]
    grad_gain_attn, grad_gain_mlp, grad_gain_out, grad_taps, grad_beta_matrix = parts
    return (
        layer_out[None],
        grad_inputs,
        grad_gain_attn,
        grad_query_matrix.astype(f32),
        grad_key_matrix.astype(f32),
        grad_value_matrix.astype(f32),
        grad_beta_matrix,
        grad_taps,
        grad_gain_out,
        grad_out_matrix.astype(f32),
        grad_gain_mlp,
        grad_gate_matrix.astype(f32),
        grad_up_matrix.astype(f32),
        jnp.transpose(grad_down_t).astype(f32),
    )


def solution(mesh):
    vector = P("fsdp")
    rows = P("fsdp", None)
    columns = P(None, "fsdp")
    tokens = P("fsdp", "seq", None)
    return jax.shard_map(
        local,
        mesh=mesh,
        in_specs=(
            tokens,
            vector,
            rows,
            rows,
            rows,
            rows,
            columns,
            vector,
            rows,
            vector,
            rows,
            rows,
            columns,
            tokens,
        ),
        out_specs=(
            tokens,
            tokens,
            vector,
            rows,
            rows,
            rows,
            rows,
            columns,
            vector,
            rows,
            vector,
            rows,
            rows,
            columns,
        ),
        check_vma=False,
    )
```

time: 3560 us -> 732 us (0.21)
  matrix products: 1750 us -> 160 us
  waiting for transfers between devices: 836 us -> 0.04 us
  Pallas kernels: 0 us -> 479 us
  local copies, waits for them, and re-layouts: 408 us -> 32.9 us
  blocking collectives: 241 us -> 0 us
  other arithmetic: 195 us -> 29.3 us
  loops' own time: 36.2 us -> 0 us
    dot_general x4440 -> x30, matrix products: 1750 us -> 160 us  [the longest x8 55.3 us: nn(): lax.dot_general(left_side, right_side, (((1,), (0,)), ((), ())), preferre...]
    reduce_scatter x8 -> x0, waiting for transfers between devices: 776 us -> none  [the longest x1 195 us: local(): lax.psum_scatter(grad_gate_matrix, 'fsdp', scatter_dimension=0, tiled=True)]
    pallas_call x0 -> x8, Pallas kernels: none -> 479 us  [the longest x2 187 us: reduce_all(): pl.pallas_call(functools.partial(reduce_kernel, arrays, count, pieces), i...]
    squeeze x320 -> x0, local copies, waits for them, and re-layouts: 224 us -> none  [recurrence(): lax.scan(jax.checkpoint(block_step), initial, (blocks(queries), blocks(ke...]
    all_gather x4 -> x0, blocking collectives: 97 us -> none  [the longest x1 30.6 us: local(): lax.all_gather(conv_taps, 'fsdp', axis=1, tiled=True)]
    all_to_all x3 -> x0, blocking collectives: 85.6 us -> none  [the longest x1 28.9 us: local(): lax.all_to_all(grad_key.astype(jnp.bfloat16), 'seq', split_axis=0, concat...]
    reduce_sum x72 -> x1, other arithmetic: 57.3 us -> 2.07 us  [norm_backward(): jnp.mean(values * values, axis=-1, keepdims=True) + epsilon]
    pad x3 -> x2, local copies, waits for them, and re-layouts: 53.4 us -> 0.02 us  [the longest x1 0.01 us: pack_shard(): return jnp.pad(flat, (0, PACK[0] * PACK[1] - flat.shape[0])).reshape(PACK)]
where the time goes in v1:
time: 732 us; the launch traced here: 721 us
  Pallas kernels  479 us (65%)
  matrix products  160 us (22%)
  local copies, waits for them, and re-layouts  32.9 us (4%)
  other arithmetic  29.3 us (4%)
  between operations  15.5 us (2%)
    pallas_call x2, Pallas kernels, reduce_all(): pl.pallas_call(functools.partial(reduce_kernel, arrays, count, pieces), i...  187 us
    pallas_call x2, Pallas kernels, gather_all(): pl.pallas_call(functools.partial(gather_kernel, arrays, count), in_specs=...  182 us
    dot_general x8, matrix products, nn(): lax.dot_general(left_side, right_side, (((1,), (0,)), ((), ())), preferre...  55.3 us
    pallas_call x1, Pallas kernels, delta_backward(): pl.pallas_call(backward_kernel, grid=(heads,), in_specs=[column, column,...  51.4 us
    dot_general x8, matrix products, tn(): lax.dot_general(left_side, right_side, (((0,), (0,)), ((), ())), preferre...  46.8 us
    dot_general x8, matrix products, nt(): lax.dot_general(left_side, right_side, (((1,), (1,)), ((), ())), preferre...  46 us
    pallas_call x1, Pallas kernels, delta_forward(): pl.pallas_call(forward_kernel, grid=(heads,), in_specs=[column, column, c...  45.4 us
    unnamed x128, local copies, waits for them, and re-layouts  28.3 us
  transfers between devices with their start and end apart: 4, of which 0 were waited for; matrix products, arithmetic and copies ran while one was open for 6% of the time, Pallas kernels for 42%

profile of v1, /device:TPU:0, one launch (start us, length us, event | category | flops | bytes accessed | tf_op | source)
XLA Modules:
  0.0 721.0 jit_solution(5457000363808715073)
XLA Ops:
  7.3 2.9 copy.74
  10.3 2.4 collective-permute-start
  13.7 63.5 %shard_map.245 = (bf16[128,256]{1,0:T(8,128)(2,1)}, bf16[1024,1024]{1,0:T(8,128)(2,1)}, bf16[1024,1024]{1,0:T(8,128)(2,1)}, bf16[1024,1024]{1,0:T(8,128)(2,1)}, bf16[1024,1024]{1,0:T(8,128)(2,1)}) custom-call(bf16[16,256]{1,0:T(8,128)(2,1)} %reshape.147.refs_0_, bf16[128,1024]{1,0:T(8,128)(2,1)} %refs_1_.2, bf16[128,1024]{1,0:T(8,128)(2,1)} %refs_2_.1, ...), custom_call_target="tpu_custom_call" | custom-call | tf_op jit(solution)/shard_map/pallas_call | solution.py:270
  80.3 2.1 fusion.10
  83.9 3.8 convolution_convert_fusion.3.v_ref
  87.7 3.8 convolution_convert_fusion.4.k_ref
  91.5 4.1 convolution_convert_fusion.5.q_ref
  95.7 45.4 %shard_map.246 = (f32[1024,1024]{1,0:T(8,128)}, bf16[1024,1024]{1,0:T(8,128)(2,1)S(1)}, bf16[1024,2048]{1,0:T(8,128)(2,1)}, bf16[1024,2048]{1,0:T(8,128)(2,1)}, ...) custom-call(bf16[1040,1024]{1,0:T(8,128)(2,1)} %convolution_convert_fusion.5.q_ref, ...), custom_call_target="tpu_custom_call" | custom-call | tf_op jit(solution)/shard_map/pallas_call | solution.py:663
  143.8 3.9 copy.81
  147.7 118.1 %shard_map.248 = (bf16[1024,2816]{1,0:T(8,128)(2,1)}, bf16[1024,2816]{1,0:T(8,128)(2,1)}, bf16[1024,2816]{1,0:T(8,128)(2,1)}) custom-call(bf16[128,2816]{1,0:T(8,128)(2,1)} %refs_0_.1, bf16[128,2816]{1,0:T(8,128)(2,1)} %refs_1_.3, bf16[128,2816]{1,0:T(8,128)(2,1)} %bitcast.201), custom_call_target="tpu_custom_call" | custom-call | tf_op jit(solution)/shard_map/pallas_call | solution.py:270
  265.8 2.1 fusion.17
  268.5 1.9 convolution_add_fusion.6
  270.4 1.8 convolution_add_fusion.5
  272.2 1.8 fusion.23
  274.9 4.7 shard_map.247
  279.7 2.6 multiply_reduce_fusion.2
  282.3 1.9 copy-done.12
  284.7 9.0 %fusion.54 = f32[1024,2816]{1,0:T(8,128)} fusion(bf16[1024,1024]{0,1:T(8,128)(2,1)S(1)} %multiply_convert_fusion.1, bf16[1024,2816]{1,0:T(8,128)(2,1)S(1)} %bitcast.231), kind=kOutput, calls=%fused_computation.130 | convolution fusion | flops 5905580032 | bytes 19398656 | tf_op jit(solution)/shard_map/dot_general | solution.py:22
  293.6 9.2 %fusion.55 = f32[1024,2816]{1,0:T(8,128)} fusion(bf16[1024,1024]{0,1:T(8,128)(2,1)S(1)} %multiply_convert_fusion.1, bf16[1024,2816]{1,0:T(8,128)(2,1)S(1)} %bitcast.227), kind=kOutput, calls=%fused_computation.131 | convolution fusion | flops 5905580032 | bytes 19398656 | tf_op jit(solution)/shard_map/dot_general | solution.py:22
  302.8 21.4 %fusion.3 = (bf16[1024,2816]{1,0:T(8,128)(2,1)}, bf16[1024,2816]{1,0:T(8,128)(2,1)}, bf16[1024,2816]{1,0:T(8,128)(2,1)}) fusion(f32[1024,2816]{1,0:T(8,128)} %fusion.54, f32[1024,2816]{1,0:T(8,128)} %fusion.55, bf16[1024,2816]{1,0:T(8,128)(2,1)} %get-tuple-element.56, bf16[1,1024,1024]{2,1,0:T(8,128)(2,1)} %param.27), kind=kOutput, calls=%fused_computation.5 | convolution fusion | flops 5948833792 | bytes 48234496 | tf_op jit(solution)/shard_map/dot_general | solution.py:22
  324.2 11.0 %convolution_convert_fusion.2 = bf16[1024,2816]{1,0:T(8,128)(2,1)} fusion(bf16[1024,1024]{0,1:T(8,128)(2,1)} %copy-done.22, bf16[1024,2816]{1,0:T(8,128)(2,1)} %get-tuple-element.125), kind=kOutput, calls=%fused_computation.19 | convolution fusion | flops 5908463616 | bytes 13631488 | tf_op jit(solution)/shard_map/dot_general | solution.py:34
  335.3 9.7 %fusion.56 = f32[1024,1024]{0,1:T(8,128)} fusion(bf16[1024,2816]{1,0:T(8,128)(2,1)S(1)} %copy-done.48, bf16[1024,2816]{1,0:T(8,128)(2,1)} %get-tuple-element.54), kind=kOutput, calls=%fused_computation.132 | convolution fusion | flops 5905580032 | bytes 15728640 | tf_op jit(solution)/shard_map/dot_general | solution.py:28
  345.0 8.3 %convolution_convert_fusion.1 = bf16[1024,2816]{1,0:T(8,128)(2,1)} fusion(bf16[1024,1024]{0,1:T(8,128)(2,1)S(1)} %copy-done.23, bf16[1024,2816]{1,0:T(8,128)(2,1)S(1)} %bitcast.235), kind=kOutput, calls=%fused_computation.18 | convolution fusion | flops 5908463616 | bytes 13631488 | tf_op jit(solution)/shard_map/dot_general | solution.py:34
  353.3 8.1 %convolution_convert_fusion = bf16[2816,1024]{0,1:T(8,128)(2,1)} fusion(bf16[1024,2816]{1,0:T(8,128)(2,1)S(1)} %bitcast.233, bf16[1,1024,1024]{2,1,0:T(8,128)(2,1)S(1)} %copy-done.21), kind=kOutput, calls=%fused_computation.17 | convolution fusion | flops 5908463616 | bytes 13631488 | tf_op jit(solution)/shard_map/dot_general | solution.py:34
  361.4 9.6 %multiply_reduce_fusion = (bf16[1024]{0:T(1024)(128)(2,1)S(1)}, f32[1024]{0:T(1024)S(1)}, f32[1024,1024]{0,1:T(8,128)S(1)}) fusion(f32[1024,1024]{0,1:T(8,128)S(1)} %copy-done.13, f32[1024]{0:T(1024)S(1)} %add_rsqrt_fusion.2, f32[1024]{0:T(1024)S(1)} %get-tuple-element.130, f32[1024,1024]{0,1:T(8,128)} %fusion.56, ...), kind=kOutput, calls=%fused_computation.30 | convolution fusion | flops 5912918016 | bytes 24131584 | tf_op jit(solution)/shard_map/dot_general | solution.py:28
  372.6 2.4 convolution_convert_fusion.10.grad_ref
  376.3 9.2 %shard_map.249 = (bf16[1024,1024]{1,0:T(8,128)(2,1)S(1)}, f32[8,128,128]{2,1,0:T(8,128)}, f32[1,128]{1,0:T(1,128)S(1)}) custom-call(f32[1024,1024]{1,0:T(8,128)S(1)} %copy-done.1, bf16[1024,1024]{1,0:T(8,128)(2,1)S(1)} %get-tuple-element.51.carry_ref, f32[8,128,128]{2,1,0:T(8,128)S(1)} %fusion.38.state_ref, bf16[1,128]{1,0:T(2,128)(2,1)S(1)} %reshape_reshape.14.gain_ref, ...), custom_call_target="tpu_custom_call" | custom-call | tf_op jit(solution)/shard_map/pallas_call | solution.py:749
  387.0 121.7 %shard_map.252 = (bf16[128,2816]{1,0:T(8,128)(2,1)}, bf16[128,2816]{1,0:T(8,128)(2,1)}, bf16[128,2816]{1,0:T(8,128)(2,1)}) custom-call(bf16[8,128,2816]{2,1,0:T(8,128)(2,1)} %bitcast.194, bf16[8,128,2816]{2,1,0:T(8,128)(2,1)} %bitcast.195, bf16[8,128,2816]{2,1,0:T(8,128)(2,1)} %bitcast.196), custom_call_target="tpu_custom_call" | custom-call | tf_op jit(solution)/shard_map/pallas_call | solution.py:514
  514.1 11.5 %fusion.18 = bf16[1,1024,1024]{1,2,0:T(8,128)(2,1)} fusion(f32[1024,1024]{0,1:T(8,128)} %copy-done.12, bf16[1024,2816]{1,0:T(8,128)(2,1)} %get-tuple-element.126, bf16[1024,2816]{1,0:T(8,128)(2,1)} %get-tuple-element.56), kind=kOutput, calls=%fused_computation.41 | convolution fusion | flops 5907677184 | bytes 17825792 | tf_op jit(solution)/shard_map/dot_general | solution.py:28
  525.5 4.1 copy.97
  529.6 5.9 convolution_convert_fusion.6
  535.6 2.3 convolution_add_fusion.3
  537.8 2.2 convolution_add_fusion.2
  540.0 2.2 fusion.22
  543.2 51.4 %shard_map.250 = (bf16[1024,1024]{1,0:T(8,128)(2,1)}, bf16[1024,1024]{1,0:T(8,128)(2,1)}, bf16[1024,1024]{1,0:T(8,128)(2,1)}, f32[8,3,16,128]{3,2,1,0:T(8,128)},...) custom-call(bf16[1040,1024]{1,0:T(8,128)(2,1)} %convolution_convert_fusion.5.q_ref, ...), custom_call_target="tpu_custom_call" | custom-call | tf_op jit(solution)/shard_map/pallas_call | solution.py:909
  596.1 1.9 convolution_convert_fusion.12
  601.0 4.7 fusion.57
  605.8 3.8 convolution_convert_fusion.9
  609.7 2.4 fusion.58
  612.0 3.7 convolution_convert_fusion.8
  615.8 2.4 fusion.59
  618.2 4.1 convolution_convert_fusion.7
  622.3 3.3 fusion.16
  626.4 65.1 %shard_map.251 = (bf16[16,256]{1,0:T(8,128)(2,1)}, bf16[128,1024]{1,0:T(8,128)(2,1)}, bf16[128,1024]{1,0:T(8,128)(2,1)}, bf16[128,1024]{1,0:T(8,128)(2,1)}, bf16[128,1024]{1,0:T(8,128)(2,1)}) custom-call(bf16[8,16,256]{2,1,0:T(8,128)(2,1)} %bitcast.212, bf16[8,128,1024]{2,1,0:T(8,128)(2,1)} %bitcast.209, bf16[8,128,1024]{2,1,0:T(8,128)(2,1)} %bitcast.210, ...), custom_call_target="tpu_custom_call" | custom-call | tf_op jit(solution)/shard_map/pallas_call | solution.py:514
  693.4 1.8 convert_element_type.232
  695.2 1.8 convert_element_type.233
  701.9 6.5 fusion.15
  708.4 5.3 copy.98
  (191 shorter events, 32.9 us)
Async XLA Ops:
  7.2 5.5 copy-start.34
  7.2 5.7 copy-start.33
  7.2 5.8 copy-start.35
  7.2 5.7 copy-start.37
  7.2 5.7 copy-start.36
  7.2 261.2 %all-gather.5.cloned.1.call-start = ((), (), s32[]{:S(2)}) async-start(), calls=%async_computation | async-start | bytes 5242880 | tf_op jit(solution)/shard_map/all_gather | solution.py:1020
  10.1 72.2 %copy-start.9 = (bf16[1,1024,1024]{1,2,0:T(8,128)(2,1)}, bf16[1,1024,1024]{1,2,0:T(8,128)(2,1)S(1)}, u32[]{:S(2)}) copy-start(bf16[1,1024,1024]{1,2,0:T(8,128)(2,1)S(1)} %copy.74) | copy-start | bytes 6291460
  10.3 68.4 %collective-permute-start = (bf16[16,1024]{0,1:T(8,128)(2,1)S(1)}, bf16[16,1024]{0,1:T(8,128)(2,1)S(1)}, u32[]{:S(2)}, u32[]{:S(2)}) collective-permute-start(bf16[16,1024]{0,1:T(8,128)(2,1)S(1)} %slice_bitcast_fusion.13), channel_id=1, source_target_pairs={{0,8},{8,16},{16,24},{1,9},{9,17},{17,25},{2,10},{10,18},{18,26},{... | collective-permute-start | bytes 98312 | tf_op jit(solution)/shard_map/ppermute | solution.py:1003
  78.1 5.8 copy-start.30
  78.6 5.3 copy-start.25
  78.6 17.0 %copy-start.8 = (bf16[4,3,8,128]{3,0,1,2:T(4,128)(2,1)}, bf16[4,3,8,128]{3,0,1,2:T(4,128)(2,1)S(1)}, u32[]{:S(2)}) copy-start(bf16[4,3,8,128]{3,0,1,2:T(4,128)(2,1)S(1)} %copy.124) | copy-start | bytes 73732
  82.4 9.1 %copy-start.15 = (bf16[1040,1024]{0,1:T(8,128)(2,1)}, bf16[1040,1024]{0,1:T(8,128)(2,1)S(1)}, u32[]{:S(2)}) copy-start(bf16[1040,1024]{0,1:T(8,128)(2,1)S(1)} %fusion.10) | copy-start | bytes 6389764
  83.9 11.8 %copy-start.7 = (bf16[1024,8]{1,0:T(8,128)(2,1)}, bf16[1024,8]{1,0:T(8,128)(2,1)S(1)}, u32[]{:S(2)}) copy-start(bf16[1024,8]{1,0:T(8,128)(2,1)S(1)} %convolution_convert_fusion.11.logit_ref) | copy-start | bytes 49156
  87.7 3.8 copy-start.42
  95.7 46.9 %copy-start.27 = (bf16[2816,128]{1,0:T(8,128)(2,1)S(1)}, bf16[2816,128]{1,0:T(8,128)(2,1)}, u32[]{:S(2)}) copy-start(bf16[2816,128]{1,0:T(8,128)(2,1)} %param.26) | copy-start | bytes 2162692
  142.5 393.1 %all-gather.7.cloned.1.call-start = ((), (), s32[]{:S(2)}) async-start(), calls=%async_computation.1 | async-start | bytes 2621440 | tf_op jit(solution)/shard_map/all_gather | solution.py:1059
  268.5 6.5 copy-start
  274.3 100.7 %copy-start.2 = (f32[8,128,128]{2,1,0:T(8,128)}, f32[8,128,128]{2,1,0:T(8,128)S(1)}, u32[]{:S(2)}) copy-start(f32[8,128,128]{2,1,0:T(8,128)S(1)} %fusion.38.state_ref) | copy-start | bytes 1572868
  274.9 4.7 copy-start.10
  274.9 4.7 copy-start.43
  279.6 5.0 slice-start.4
  279.6 5.0 slice-start.5
  284.2 9.4 %slice-start = ((s8[5767168]{0:T(1024)(128)(4,1)}), s8[4194304]{0:T(1024)(128)(4,1)S(1)}, s32[]{:S(2)}) async-start(s8[5767168]{0:T(1024)(128)(4,1)} %bitcast.226), calls=%async_computation.2 | async-start | bytes 8388608
  284.6 9.0 %copy-start.22 = (bf16[1024,1024]{0,1:T(8,128)(2,1)}, bf16[1024,1024]{0,1:T(8,128)(2,1)S(1)}, u32[]{:S(2)}) copy-start(bf16[1024,1024]{0,1:T(8,128)(2,1)S(1)} %multiply_convert_fusion.1) | copy-start | bytes 6291460
  284.6 9.0 %slice-start.1 = ((s8[5767168]{0:T(1024)(128)(4,1)}), s8[1572864]{0:T(1024)(128)(4,1)S(1)}, s32[]{:S(2)}) async-start(s8[5767168]{0:T(1024)(128)(4,1)} %bitcast.226), calls=%async_computation.3 | async-start | bytes 3145728
  324.2 11.0 %copy-start.48 = (bf16[1024,2816]{1,0:T(8,128)(2,1)S(1)}, bf16[1024,2816]{1,0:T(8,128)(2,1)}, u32[]{:S(2)}) copy-start(bf16[1024,2816]{1,0:T(8,128)(2,1)} %get-tuple-element.125) | copy-start | bytes 17301508
  324.2 20.7 %slice-start.8 = ((s8[5767168]{0:T(1024)(128)(4,1)}), s8[4194304]{0:T(1024)(128)(4,1)S(1)}, s32[]{:S(2)}) async-start(s8[5767168]{0:T(1024)(128)(4,1)} %bitcast.234), calls=%async_computation.10 | async-start | bytes 8388608
  324.2 29.1 %slice-start.6 = ((s8[5767168]{0:T(1024)(128)(4,1)}), s8[4194304]{0:T(1024)(128)(4,1)S(1)}, s32[]{:S(2)}) async-start(s8[5767168]{0:T(1024)(128)(4,1)} %bitcast.232), calls=%async_computation.8 | async-start | bytes 8388608
  335.2 9.7 %copy-start.23 = (bf16[1024,1024]{0,1:T(8,128)(2,1)S(1)}, bf16[1024,1024]{0,1:T(8,128)(2,1)}, u32[]{:S(2)}) copy-start(bf16[1024,1024]{0,1:T(8,128)(2,1)} %copy-done.22) | copy-start | bytes 6291460
  335.2 9.7 %slice-start.9 = ((s8[5767168]{0:T(1024)(128)(4,1)}), s8[1572864]{0:T(1024)(128)(4,1)S(1)}, s32[]{:S(2)}) async-start(s8[5767168]{0:T(1024)(128)(4,1)} %bitcast.234), calls=%async_computation.11 | async-start | bytes 3145728
  335.3 18.0 %slice-start.7 = ((s8[5767168]{0:T(1024)(128)(4,1)}), s8[1572864]{0:T(1024)(128)(4,1)S(1)}, s32[]{:S(2)}) async-start(s8[5767168]{0:T(1024)(128)(4,1)} %bitcast.232), calls=%async_computation.9 | async-start | bytes 3145728
  345.0 8.3 %copy-start.21 = (bf16[1,1024,1024]{2,1,0:T(8,128)(2,1)S(1)}, bf16[1,1024,1024]{2,1,0:T(8,128)(2,1)}, u32[]{:S(2)}) copy-start(bf16[1,1024,1024]{2,1,0:T(8,128)(2,1)} %param.27) | copy-start | bytes 6291460
  345.0 16.4 %slice-start.2 = ((s8[5767168]{0:T(1024)(128)(4,1)}), s8[4194304]{0:T(1024)(128)(4,1)S(1)}, s32[]{:S(2)}) async-start(s8[5767168]{0:T(1024)(128)(4,1)} %bitcast.228), calls=%async_computation.4 | async-start | bytes 8388608
  353.3 8.1 %copy-start.13 = (f32[1024,1024]{0,1:T(8,128)S(1)}, f32[1024,1024]{0,1:T(8,128)}, u32[]{:S(2)}) copy-start(f32[1024,1024]{0,1:T(8,128)} %copy-done.12) | copy-start | bytes 12582916
  353.3 8.1 %slice-start.3 = ((s8[5767168]{0:T(1024)(128)(4,1)}), s8[1572864]{0:T(1024)(128)(4,1)S(1)}, s32[]{:S(2)}) async-start(s8[5767168]{0:T(1024)(128)(4,1)} %bitcast.228), calls=%async_computation.5 | async-start | bytes 3145728
  361.4 9.6 %copy-start.18 = (bf16[1,1024,1024]{1,2,0:T(8,128)(2,1)S(1)}, bf16[1,1024,1024]{1,2,0:T(8,128)(2,1)}, u32[]{:S(2)}) copy-start(bf16[1,1024,1024]{1,2,0:T(8,128)(2,1)} %copy.81) | copy-start | bytes 6291460
  508.7 4.1 copy-start.28
  525.5 4.1 copy-start.4
  535.6 6.7 copy-start.20
  543.2 52.9 %copy-start.16 = (bf16[1040,1024]{0,1:T(8,128)(2,1)S(1)}, bf16[1040,1024]{0,1:T(8,128)(2,1)}, u32[]{:S(2)}) copy-start(bf16[1040,1024]{0,1:T(8,128)(2,1)} %copy-done.15) | copy-start | bytes 6389764
  594.6 4.8 collective-permute-start.1
  601.0 4.8 copy-start.47
  605.8 3.9 copy-start.41
  618.2 4.1 copy-start.11
  618.2 4.1 copy-start.24
  618.2 4.1 copy-start.26
  618.2 4.1 copy-start.31
  618.2 4.1 copy-start.32
  (15 other events, 39.9 us)
Sparse Core Ops, SparseCore 0:
  142.6 35.6 all-gather.4
  387.1 30.4 all-gather.6

commit v2 on v1

v2 whole, which is shorter than its diff:
```python
import functools

import jax
import jax.numpy as jnp
from jax import lax
from jax.experimental import pallas as pl
from jax.experimental.pallas import tpu as pltpu
from jax.sharding import PartitionSpec as P

CHUNK = 256
HALO = 16
TAPS = 4
MIB = 1024 * 1024

highest = lax.Precision.HIGHEST
epsilon = 1e-06
f32 = jnp.float32
bf16 = jnp.bfloat16


def nn(left_side, right_side):
    return lax.dot_general(
        left_side, right_side, (((1,), (0,)), ((), ())), preferred_element_type=f32
    )


def nt(left_side, right_side):
    return lax.dot_general(
        left_side, right_side, (((1,), (1,)), ((), ())), preferred_element_type=f32
    )


def tn(left_side, right_side):
    return lax.dot_general(
        left_side, right_side, (((0,), (0,)), ((), ())), preferred_element_type=f32
    )


def rms_scale(values, gain_vec):
    return (
        values * lax.rsqrt(jnp.mean(values * values, axis=-1, keepdims=True) + epsilon) * gain_vec
    )


def norm_backward(values, gain_vec, grad_out):
    scaling = lax.rsqrt(jnp.mean(values * values, axis=-1, keepdims=True) + epsilon)
    unit_rows = values * scaling
    gain_grad = jnp.sum(grad_out * unit_rows, axis=0)
    scaled_grad = grad_out * gain_vec
    input_grad = scaling * (
        scaled_grad - unit_rows * jnp.mean(scaled_grad * unit_rows, axis=-1, keepdims=True)
    )
    return (input_grad, gain_grad)


MESH = pl.DeviceIdType.MESH


class Place:
    def __init__(self, count):
        self.count = count
        self.sides = 2 if count % 2 == 0 else 1
        self.length = count // self.sides
        self.position = lax.axis_index("seq")
        self.index = lax.axis_index("fsdp")
        self.core = lax.rem(self.position, 2)
        self.chip = lax.div(self.position, 2)
        self.side = lax.rem(self.index, self.sides)
        self.spot = lax.div(self.index, self.sides)

    def sibling(self):
        return {"seq": self.position + 1 - 2 * self.core, "fsdp": self.index}

    def across(self):
        return {"seq": lax.rem(self.position + 2, 4), "fsdp": self.index}

    def partner(self):
        return {"seq": self.position, "fsdp": self.spot * 2 + 1 - self.side}

    def ahead(self, step):
        spot = lax.rem(self.spot + step, self.length)
        return {"seq": self.position, "fsdp": spot * self.sides + self.side}

    def shard(self, spot, side):
        return spot * self.sides + side

    def behind(self, step):
        return lax.rem(self.spot + self.length - step, self.length)

    def greet_all(self):
        self.greet(False, True)

    def greet(self, across, sequence=False):
        barrier = pltpu.get_barrier_semaphore()
        total = self.length - 1

        def signal(device):
            pl.semaphore_signal(barrier, inc=1, device_id=device, device_id_type=MESH)

        def one(step, carry):
            signal(self.ahead(step))
            return carry

        lax.fori_loop(1, self.length, one, 0)
        if sequence:
            for hop in range(1, 4):
                signal({"seq": lax.rem(self.position + hop, 4), "fsdp": self.index})
            total += 3
        else:
            signal(self.sibling())
            total += 1
        if self.sides == 2:
            signal(self.partner())
            total += 1
        if across:
            signal(self.across())
            total += 1
        pl.semaphore_wait(barrier, total)


def remote(source, target, send, recv, device):
    return pltpu.make_async_remote_copy(
        src_ref=source,
        dst_ref=target,
        send_sem=send,
        recv_sem=recv,
        device_id=device,
        device_id_type=MESH,
    )


def steps(first, last, body):
    def one(step, carry):
        body(step)
        return carry

    lax.fori_loop(first, last, one, 0)


class Reduce:
    def __init__(self, count, pieces, sources, outs, buffers, sems):
        self.place = Place(count)
        self.pieces, self.sources, self.outs = pieces, sources, outs
        self.total, self.core_in, self.side_in, self.line_in, self.across_in, self.done = buffers
        (
            self.core_sem,
            self.load_sem,
            self.side_sem,
            self.line_sem,
            self.across_sem,
            self.last_sem,
            self.store_sem,
        ) = sems

    @staticmethod
    def plan(widths, limit):
        pieces = []
        for a, width in enumerate(widths):
            tiles = max(width // 256, 1)
            parts = -(-tiles * 128 // limit)
            offset = 0
            for part in range(parts):
                wide = (tiles // parts + (1 if part < tiles % parts else 0)) * 128
                pieces.append((a, offset, wide))
                offset += wide
        return pieces

    @staticmethod
    def scratch(count, pieces, depths):
        sides = 2 if count % 2 == 0 else 1
        length = count // sides
        pairs = [(depths[a], wide) for a, _, wide in pieces]
        number = len(pieces)

        def stack(lead):
            return [pltpu.VMEM(lead + pair, bf16) for pair in pairs]

        shapes = (
            stack((count,)) + stack((count,)) + stack((length,)) + stack((length,))
            + stack(()) + stack(())
        )
        sems = [
            pltpu.SemaphoreType.DMA((number, 2)),
            pltpu.SemaphoreType.DMA((number,)),
            pltpu.SemaphoreType.DMA((number, 2, length)),
            pltpu.SemaphoreType.DMA((number, 2, length)),
            pltpu.SemaphoreType.DMA((number, 2)),
            pltpu.SemaphoreType.DMA((number, 2)),
            pltpu.SemaphoreType.DMA((number,)),
        ]
        return shapes + sems

    @staticmethod
    def split(refs, number):
        buffers = [refs[i * number : (i + 1) * number] for i in range(6)]
        return buffers, refs[6 * number :]

    def columns(self, p, core):
        a, offset, wide = self.pieces[p]
        width = self.sources[a].shape[2] // 2
        return a, pl.ds(pl.multiple_of(core * width + offset, 128), wide)

    def to_sibling(self, p):
        a, columns = self.columns(p, 1 - self.place.core)
        return remote(
            self.sources[a].at[:, :, columns],
            self.core_in[p],
            self.core_sem.at[p, 0],
            self.core_sem.at[p, 1],
            self.place.sibling(),
        )

    def load(self, p):
        a, columns = self.columns(p, self.place.core)
        return pltpu.make_async_copy(
            self.sources[a].at[:, :, columns], self.total[p], self.load_sem.at[p]
        )

    def to_side(self, p, spot):
        place = self.place
        return remote(
            self.total[p].at[place.shard(spot, 1 - place.side)],
            self.side_in[p].at[spot],
            self.side_sem.at[p, 0, spot],
            self.side_sem.at[p, 1, spot],
            place.partner(),
        )

    def to_line(self, p, step):
        place = self.place
        spot = lax.rem(place.spot + step, place.length)
        return remote(
            self.total[p].at[place.shard(spot, place.side)],
            self.line_in[p].at[step],
            self.line_sem.at[p, 0, step],
            self.line_sem.at[p, 1, step],
            place.ahead(step),
        )

    def to_across(self, p):
        return remote(
            self.done[p],
            self.across_in[p],
            self.across_sem.at[p, 0],
            self.across_sem.at[p, 1],
            self.place.across(),
        )

    def target(self, p, core):
        a, columns = self.columns(p, core)
        return self.outs[a].at[:, columns]

    def to_result(self, p, arriving):
        core = 1 - self.place.core if arriving else self.place.core
        return remote(
            self.across_in[p],
            self.target(p, core),
            self.last_sem.at[p, 0],
            self.last_sem.at[p, 1],
            self.place.sibling(),
        )

    def store(self, p):
        return pltpu.make_async_copy(
            self.across_in[p], self.target(p, self.place.core), self.store_sem.at[p]
        )

    def start(self, p):
        self.to_sibling(p).start()
        self.load(p).start()

    def stage_core(self, p):
        place = self.place
        self.load(p).wait()
        self.to_sibling(p).wait_recv()
        if place.sides == 2:

            def one(step):
                spot = lax.rem(place.spot + step, place.length)
                shard = place.shard(spot, 1 - place.side)
                self.total[p][shard] = (
                    self.total[p][shard].astype(f32) + self.core_in[p][shard].astype(f32)
                ).astype(bf16)
                self.to_side(p, spot).start()

            steps(1, place.length + 1, one)

    def stage_side(self, p):
        place = self.place

        def one(step):
            spot = lax.rem(place.spot + step, place.length)
            shard = place.shard(spot, place.side)
            total = self.total[p][shard].astype(f32) + self.core_in[p][shard].astype(f32)
            if place.sides == 2:
                self.to_side(p, spot).wait_recv()
                total = total + self.side_in[p][spot].astype(f32)
            self.total[p][shard] = total.astype(bf16)

        def send(step):
            one(step)
            self.to_line(p, step).start()

        steps(1, place.length, send)
        one(0)

    def stage_line(self, p):
        place = self.place
        self.done[p][...] = self.total[p][place.index]

        def one(step):
            self.to_line(p, step).wait_recv()

        steps(1, place.length, one)
        total = self.total[p][place.index].astype(f32)
        if place.length <= 8:
            for step in range(1, place.length):
                total = total + self.line_in[p][step].astype(f32)
        else:
            total = lax.fori_loop(
                1,
                place.length,
                lambda step, carry: carry + self.line_in[p][step].astype(f32),
                total,
            )
        self.done[p][...] = total.astype(bf16)
        self.to_across(p).start()

    def stage_across(self, p):
        copy = self.to_across(p)
        copy.wait_recv()
        self.across_in[p][...] = (
            self.across_in[p][...].astype(f32) + self.done[p][...].astype(f32)
        ).astype(bf16)
        self.to_result(p, False).start()
        self.store(p).start()

    def finish(self, p):
        place = self.place
        self.to_sibling(p).wait_send()
        if place.sides == 2:
            steps(0, place.length, lambda spot: self.to_side(p, spot).wait_send())
        steps(1, place.length, lambda step: self.to_line(p, step).wait_send())
        self.to_across(p).wait_send()
        self.to_result(p, False).wait_send()
        self.to_result(p, True).wait_recv()
        self.store(p).wait()


def reduce_kernel(arrays, count, pieces, *refs):
    buffers, sems = Reduce.split(refs[2 * arrays :], len(pieces))
    reduce = Reduce(count, pieces, refs[:arrays], refs[arrays : 2 * arrays], buffers, sems)
    reduce.place.greet(True)
    number = len(pieces)
    for p in range(number):
        reduce.start(p)
    stages = (reduce.stage_core, reduce.stage_side, reduce.stage_line, reduce.stage_across)
    for turn in range(number + len(stages) - 1):
        for behind, stage in enumerate(stages):
            if 0 <= turn - behind < number:
                stage(turn - behind)
    for p in range(number):
        reduce.finish(p)


def reduce_all(sources, collective_id, limit=768):
    count = lax.axis_size("fsdp")
    arrays = len(sources)
    views = [s.reshape(count, s.shape[0] // count, s.shape[1]) for s in sources]
    pieces = Reduce.plan([s.shape[1] for s in sources], limit)
    anywhere = pl.BlockSpec(memory_space=pl.ANY)
    return pl.pallas_call(
        functools.partial(reduce_kernel, arrays, count, pieces),
        in_specs=[anywhere] * arrays,
        out_specs=[anywhere] * arrays,
        out_shape=[jax.ShapeDtypeStruct(v.shape[1:], bf16) for v in views],
        scratch_shapes=Reduce.scratch(count, pieces, [v.shape[1] for v in views]),
        compiler_params=pltpu.CompilerParams(
            collective_id=collective_id, has_side_effects=True, vmem_limit_bytes=60 * MIB
        ),
    )(*views)


class Gather:
    SEMS = 6

    def __init__(self, count, pieces, shards, outs, sems):
        self.place = Place(count)
        self.pieces, self.shards, self.outs = pieces, shards, outs
        self.line_sem, self.side_sem, self.core_sem, self.across_sem, self.relay_sem, self.own = (
            sems
        )

    @staticmethod
    def scratch(pieces, count):
        length = count // 2 if count % 2 == 0 else count
        number = len(pieces)
        slots = 2 * length if max(piece[3] for piece in pieces) > 1 else 1
        return [
            pltpu.SemaphoreType.DMA((number, 2, length)),
            pltpu.SemaphoreType.DMA((number, 2, length)),
            pltpu.SemaphoreType.DMA((number, 2, slots)),
            pltpu.SemaphoreType.DMA((number, 2, slots)),
            pltpu.SemaphoreType.DMA((number, 2, slots)),
            pltpu.SemaphoreType.DMA((number,)),
        ]

    def portion(self, k, core, chip):
        parts = self.pieces[k][3]
        if parts == 1:
            return 0
        return core if parts == 2 else 2 * chip + core

    def region(self, k, shard, core, chip):
        a, offset, width, parts = self.pieces[k]
        depth = self.shards[a].shape[0]
        rows = depth // parts
        first = shard * depth + self.portion(k, core, chip) * rows
        return self.outs[a].at[pl.ds(pl.multiple_of(first, 16), rows), pl.ds(offset, width)]

    def source(self, k):
        p = self.place
        a, offset, width, parts = self.pieces[k]
        rows = self.shards[a].shape[0] // parts
        first = self.portion(k, p.core, p.chip) * rows
        return self.shards[a].at[pl.ds(pl.multiple_of(first, 16), rows), pl.ds(offset, width)]

    def line(self, k, step, arriving=False):
        p = self.place
        shard = p.shard(p.behind(step), p.side) if arriving else p.index
        target = self.region(k, shard, p.core, p.chip)
        return remote(
            target if arriving else self.source(k),
            target,
            self.line_sem.at[k, 0, step],
            self.line_sem.at[k, 1, step],
            p.ahead(step),
        )

    def side(self, k, step, arriving=False, own=False):
        p = self.place
        shard = p.shard(p.behind(step), 1 - p.side if arriving else p.side)
        target = self.region(k, shard, p.core, p.chip)
        return remote(
            self.source(k) if own else target,
            target,
            self.side_sem.at[k, 0, step],
            self.side_sem.at[k, 1, step],
            p.partner(),
        )

    def cross(self, k, step, other, sems, core, chip, device):
        p = self.place
        shard = p.shard(p.behind(step), 1 - p.side if other else p.side)
        target = self.region(k, shard, core, chip)
        slot = 2 * step + (1 if other else 0)
        return remote(target, target, sems.at[k, 0, slot], sems.at[k, 1, slot], device)

    def core(self, k, step, other, arriving=False):
        p = self.place
        core = 1 - p.core if arriving else p.core
        return self.cross(k, step, other, self.core_sem, core, p.chip, p.sibling())

    def across(self, k, step, other, arriving=False):
        p = self.place
        chip = 1 - p.chip if arriving else p.chip
        return self.cross(k, step, other, self.across_sem, p.core, chip, p.across())

    def relay(self, k, step, other, arriving=False):
        p = self.place
        core = 1 - p.core if arriving else p.core
        return self.cross(k, step, other, self.relay_sem, core, 1 - p.chip, p.sibling())

    def keep(self, k):
        a, offset, width, _ = self.pieces[k]
        depth = self.shards[a].shape[0]
        rows = pl.ds(pl.multiple_of(self.place.index * depth, 16), depth)
        columns = pl.ds(offset, width)
        return pltpu.make_async_copy(
            self.shards[a].at[:, columns], self.outs[a].at[rows, columns], self.own.at[k]
        )

    def hand(self, k, step, other):
        parts = self.pieces[k][3]
        if parts == 4:
            self.across(k, step, other).start()
        if parts > 1:
            self.core(k, step, other).start()

    def start(self, k):
        steps(1, self.place.length, lambda step: self.line(k, step).start())
        if self.place.sides == 2:
            self.side(k, 0, own=True).start()
        self.keep(k).start()

    def forward(self, k):
        def one(step):
            self.line(k, step, True).wait_recv()
            if self.place.sides == 2:
                self.side(k, step).start()
            self.hand(k, step, False)

        steps(1, self.place.length, one)

    def spread(self, k):
        def one(step):
            self.side(k, step, True).wait_recv()
            self.hand(k, step, True)

        if self.place.sides == 2:
            steps(0, self.place.length, one)

    def each(self, body):
        steps(1, self.place.length, lambda step: body(step, False))
        if self.place.sides == 2:
            steps(0, self.place.length, lambda step: body(step, True))

    def exchange(self, k):
        def one(step, other):
            self.across(k, step, other, True).wait_recv()
            self.relay(k, step, other).start()

        if self.pieces[k][3] == 4:
            self.each(one)

    def arrive(self, k):
        parts = self.pieces[k][3]

        def one(step, other):
            self.core(k, step, other, True).wait_recv()
            if parts == 4:
                self.relay(k, step, other, True).wait_recv()

        self.keep(k).wait()
        if parts > 1:
            self.each(one)

    def sent(self, k):
        parts = self.pieces[k][3]

        def one(step, other):
            self.core(k, step, other).wait_send()
            if parts == 4:
                self.across(k, step, other).wait_send()
                self.relay(k, step, other).wait_send()

        steps(1, self.place.length, lambda step: self.line(k, step).wait_send())
        if self.place.sides == 2:
            steps(0, self.place.length, lambda step: self.side(k, step).wait_send())
        if parts > 1:
            self.each(one)

    def events(self, tiles, urgent, ahead=3):
        made = []
        line = side = across = 0.0
        hop = 8.0
        number = len(self.pieces)
        for k in range(number):
            parts = self.pieces[k][3]
            margin = 8.0 if k < urgent else 30.0
            load = tiles[k] * (2 if parts == 4 else 4)
            line = line + load
            side = max(side + load, line + load / 4 + hop)
            last = side
            made.append((line + hop, k, 0))
            made.append((side + hop, k, 1))
            if parts == 4:
                across = max(across + 3.5 * tiles[k], side + tiles[k] / 2 + hop)
                last = across
                made.append((across + hop + margin, k, 2))
            wait = 0.0 if k < urgent else 2 * margin
            made.append((last + 2 * hop + wait + (margin if parts == 4 else 0.0), k, 3))
        made.sort()

        def action(k, kind):
            if kind == 0:
                self.forward(k)
                if k + ahead < number:
                    self.start(k + ahead)
            else:
                (self.spread, self.exchange, self.arrive)[kind - 1](k)

        return [(when, k, kind, functools.partial(action, k, kind)) for when, k, kind in made]


PACK = (16, 512)


def pack_small(gains, taps):
    count = taps.shape[0]

    def fit(values, rows):
        values = values.reshape(count, -1, values.shape[-1]).astype(bf16)
        return jnp.pad(
            values, ((0, 0), (0, rows - values.shape[1]), (0, PACK[1] - values.shape[2]))
        )

    rows = [fit(gains[0], 1), fit(gains[1], 1), fit(gains[2], 2), fit(taps, PACK[0] - 4)]
    return jnp.concatenate(rows, axis=1).reshape(count * PACK[0], PACK[1])


def unpack_small(packed, shapes):
    packed = packed.reshape(-1, PACK[0], PACK[1])
    gains = [packed[:, row, : shape[0]] for row, shape in enumerate(shapes[:3])]
    return gains + [packed[:, 4 : 4 + shapes[3][0], : shapes[3][1]]]


def place_rows(packed, count, width):
    if width % 128 == 0:
        return jnp.concatenate(
            [packed[s * PACK[0] : (s + 1) * PACK[0], :width] for s in range(count)], axis=1
        )
    total = count * width
    row = lax.broadcasted_iota(jnp.int32, (PACK[1], total), 0)
    col = lax.broadcasted_iota(jnp.int32, (PACK[1], total), 1)
    pick = jnp.where(lax.rem(col, width) == row, 1.0, 0.0).astype(bf16)
    wide = nn(packed.astype(bf16), pick)
    row = lax.broadcasted_iota(jnp.int32, wide.shape, 0)
    col = lax.broadcasted_iota(jnp.int32, wide.shape, 1)
    wide = jnp.where(lax.div(row, PACK[0]) == lax.div(col, width), wide, 0.0).astype(bf16)
    row = lax.broadcasted_iota(jnp.int32, (PACK[0], count * PACK[0]), 0)
    col = lax.broadcasted_iota(jnp.int32, (PACK[0], count * PACK[0]), 1)
    fold = jnp.where(lax.rem(col, PACK[0]) == row, 1.0, 0.0).astype(bf16)
    return nn(fold, wide)


GROUP = 2
BACK = 1


def grid_indices():
    row = lax.broadcasted_iota(jnp.int32, (CHUNK, CHUNK), 0)
    col = lax.broadcasted_iota(jnp.int32, (CHUNK, CHUNK), 1)
    return row, col


def conv_pre(wide_ref, taps, rows):
    total = None
    for offset in range(TAPS):
        term = taps[offset : offset + 1, :] * wide_ref[pl.ds(HALO - TAPS + 1 + offset, rows), :]
        total = term if total is None else total + term
    return total


def sigmoid(values):
    return 1.0 / (1.0 + jnp.exp(-values))


def head_column(table, head):
    lane = lax.broadcasted_iota(jnp.int32, table.shape, 1)
    return jnp.sum(jnp.where(lane == head, table, 0.0), axis=1, keepdims=True)


ARRAYS = 7


def forward_kernel(count, pieces, mixed, heads, tap_width, *refs):
    tokens_ref = refs[0]
    shards, refs = refs[1 : 1 + ARRAYS], refs[1 + ARRAYS :]
    gathered, refs = refs[:ARRAYS], refs[ARRAYS:]
    (
        finals_ref,
        normed_ref,
        signals_ref,
        logit_ref,
        taps_ref,
        out_ref,
        carry_ref,
        fresh_ref,
        inverse_ref,
        starts_ref,
    ), refs = refs[:10], refs[10:]
    (
        tokens,
        weights,
        rates_weight,
        packed,
        all_taps,
        wide,
        level_masks,
        final,
        halo_sem,
        token_sem,
        load_sem,
        final_sem,
        *sems,
    ) = refs
    group = pl.program_id(0)
    groups = heads // GROUP
    rows = out_ref.shape[0]
    size = out_ref.shape[1] // GROUP
    span = GROUP * size
    chunks = rows // CHUNK
    levels = CHUNK.bit_length() - 1
    row, col = grid_indices()
    gather = Gather(count, pieces, shards, gathered, sems)
    place = gather.place
    tiles = [piece[2] / 128 * shards[piece[0]].shape[0] / 128 for piece in pieces]
    events = gather.events(tiles, 2 + groups)

    def halo(arriving):
        return remote(
            tokens_ref.at[pl.ds(rows - HALO, HALO), :],
            tokens.at[pl.ds(0, HALO), :],
            halo_sem.at[0],
            halo_sem.at[1],
            {"seq": lax.rem(place.position + 1, 4), "fsdp": place.index},
        )

    def load(step, slot):
        return pltpu.make_async_copy(
            gathered[mixed].at[:, pl.ds(pl.multiple_of(step * 3 * span, 128), 3 * span)],
            weights.at[slot],
            load_sem.at[slot],
        )

    per_step = 9
    plan = {}
    mark = 0
    for step in range(groups):
        for spot in range(per_step):
            now = 60.0 + (step * per_step + spot) * 5.0
            upto = mark
            for index in range(mark, len(events)):
                when, k, kind, _ = events[index]
                if spot == 0 and kind == 3 and (k == 2 + step or (step == 0 and k < 2)):
                    upto = index + 1
                elif when <= now and upto == index:
                    upto = index + 1
            plan[step, spot] = (mark, upto)
            mark = upto
    remaining = (mark, len(events))

    def run(bounds):
        for _, _, _, action in events[bounds[0] : bounds[1]]:
            action()

    def spot(number):
        for step in range(groups):
            bounds = plan[step, number]
            if bounds[1] > bounds[0]:

                @pl.when(group == step)
                def _():
                    run(bounds)

    @pl.when(group == 0)
    def _():
        own = pltpu.make_async_copy(tokens_ref, tokens.at[pl.ds(HALO, rows), :], token_sem.at[0])
        own.start()
        place.greet_all()

        @pl.when(place.position < 3)
        def _():
            halo(False).start()

        gather.start(0)
        gather.start(1)
        gather.start(2)

        @pl.when(place.position == 0)
        def _():
            tokens[pl.ds(0, HALO), :] = jnp.zeros((HALO, tokens.shape[1]), bf16)

        for level in range(levels):
            same = (row >> (level + 1)) == (col >> (level + 1))
            below = ((row >> level) & 1 == 1) & ((col >> level) & 1 == 0)
            level_masks[level] = jnp.where(same & below, 1.0, 0.0).astype(bf16)

        limit = max(i for i, event in enumerate(events) if event[1] == 0) + 1
        run((0, limit))
        copy = pltpu.make_async_copy(gathered[0], packed, token_sem.at[1])
        copy.start()
        copy.wait()
        small = packed[...].astype(f32)
        gain = place_rows(small, count, tokens.shape[1] // count)[0:1, :]
        all_taps[...] = place_rows(small, count, tap_width)[4 : 4 + TAPS, :]
        own.wait()

        @pl.when(place.position > 0)
        def _():
            halo(True).wait_recv()

        block = 208 if tokens.shape[0] % 208 == 0 else HALO

        def norm(index):
            part = pl.ds(pl.multiple_of(index * block, HALO), block)
            normed_ref[part, :] = rms_scale(tokens[part, :].astype(f32), gain).astype(bf16)

        steps(0, tokens.shape[0] // block, norm)
        run((limit, plan[0, 0][1]))
        copy = pltpu.make_async_copy(gathered[1], rates_weight, token_sem.at[1])
        copy.start()
        load(0, 0).start()
        copy.wait()
        logit_ref[...] = nn(normed_ref[pl.ds(HALO, rows), :], rates_weight[...]).astype(bf16)
        load(0, 0).wait()

    for step in range(1, groups):
        bounds = plan[step, 0]

        @pl.when(group == step)
        def _():
            run(bounds)
            load(step, 0).start()
            load(step, 0).wait()

    signals_ref[...] = nn(normed_ref[...], weights[0]).astype(bf16)
    spot(1)

    lows = [[], [], []]
    for inner in range(GROUP):
        for which in range(3):
            first = pl.multiple_of((which * heads + group * GROUP + inner) * size, 128)
            taps = all_taps[:, pl.ds(first, size)]
            taps_ref[inner, which] = taps
            wide[...] = signals_ref[:, pl.ds((inner * 3 + which) * size, size)].astype(f32)
            pre = conv_pre(wide, taps, rows)
            act = pre * sigmoid(pre)
            if which < 2:
                act = act * lax.rsqrt(jnp.sum(act * act, axis=1, keepdims=True) + epsilon)
            lows[which].append(act.astype(bf16))
        if inner == 0:
            spot(2)
    spot(3)
    logits = logit_ref[...].astype(f32)
    rates = [sigmoid(head_column(logits, group * GROUP + inner)) for inner in range(GROUP)]
    scaling = size ** (-0.5)
    eye = jnp.where(row == col, 1.0, 0.0)
    lower = row >= col

    work = [(inner, chunk) for inner in range(GROUP) for chunk in range(chunks)]

    def cut(values, item):
        inner, chunk = item
        return values[inner][chunk * CHUNK : (chunk + 1) * CHUNK]

    queries, keys, values = lows
    stricts = [(cut(rates, i) * nt(cut(keys, i), cut(keys, i))).astype(bf16) for i in work]
    results = [eye - (strict * level_masks[0]).astype(f32) for strict in stricts]
    scores = [jnp.where(lower, nt(cut(queries, i), cut(keys, i)), 0.0).astype(bf16) for i in work]
    for level in range(1, levels):
        mask = level_masks[level]
        lowered = [result.astype(bf16) for result in results]
        inners = [nn(low, strict * mask).astype(bf16) for low, strict in zip(lowered, stricts)]
        results = [
            result - nn(inner, low) for result, inner, low in zip(results, inners, lowered)
        ]
        if level in (2, 4, 6):
            spot(3 + level // 2)
    inverses = [result.astype(bf16) for result in results]
    for (inner, chunk), inverse in zip(work, inverses):
        part = slice(chunk * CHUNK, (chunk + 1) * CHUNK)
        inverse_ref[part, inner * CHUNK : (inner + 1) * CHUNK] = inverse
    spot(7)

    srow = lax.broadcasted_iota(jnp.int32, (size, size), 0)
    scol = lax.broadcasted_iota(jnp.int32, (size, size), 1)
    memories = [
        jnp.concatenate(
            [jnp.zeros((size, size), f32), jnp.where(srow == scol, 1.0, 0.0)], axis=1
        )
    ] * GROUP
    for chunk in range(chunks):
        part = slice(chunk * CHUNK, (chunk + 1) * CHUNK)
        for inner in range(GROUP):
            item = (inner, chunk)
            key_part, query_part, rate_part = cut(keys, item), cut(queries, item), cut(rates, item)
            low_memory = memories[inner].astype(bf16)
            starts_ref[inner, chunk] = low_memory
            seen = nn(key_part, low_memory)
            aim = jnp.concatenate(
                [cut(values, item).astype(f32), jnp.zeros((CHUNK, size), f32)], axis=1
            )
            aim = (rate_part * (aim - seen)).astype(bf16)
            fresh = nn(inverses[work.index(item)], aim).astype(bf16)
            fresh_ref[part, inner * 2 * size : (inner + 1) * 2 * size] = fresh
            both = scaling * (
                nn(query_part, low_memory) + nn(scores[work.index(item)], fresh)
            )
            out_ref[part, inner * size : (inner + 1) * size] = both[:, :size]
            carry_ref[part, inner * size : (inner + 1) * size] = both[:, size:].astype(bf16)
            memories[inner] = memories[inner] + tn(key_part, fresh)

    def send_final(step, hop):
        position = lax.rem(place.position + hop, 4)
        block = pl.ds(step * GROUP, GROUP)
        return remote(
            final.at[block],
            finals_ref.at[place.position, block],
            final_sem.at[0, step, hop],
            final_sem.at[1, step, hop],
            {"seq": position, "fsdp": place.index},
        )

    def keep_final(step):
        block = pl.ds(step * GROUP, GROUP)
        return pltpu.make_async_copy(
            final.at[block], finals_ref.at[place.position, block], final_sem.at[0, step, 0]
        )

    def take_final(step, hop):
        position = lax.rem(place.position + 4 - hop, 4)
        block = pl.ds(step * GROUP, GROUP)
        return remote(
            final.at[block],
            finals_ref.at[position, block],
            final_sem.at[0, step, hop],
            final_sem.at[1, step, hop],
            {"seq": position, "fsdp": place.index},
        )

    for step in range(groups):

        @pl.when(group == step)
        def _():
            for inner in range(GROUP):
                final[step * GROUP + inner] = memories[inner].astype(bf16)
            for hop in range(1, 4):
                send_final(step, hop).start()
            keep_final(step).start()

    spot(8)

    @pl.when(group == groups - 1)
    def _():
        run(remaining)
        for k in range(len(pieces)):
            gather.sent(k)
        for step in range(groups):
            for hop in range(1, 4):
                send_final(step, hop).wait_send()
                take_final(step, hop).wait_recv()
            keep_final(step).wait()

        @pl.when(place.position < 3)
        def _():
            halo(False).wait_send()


def plan_pieces(depths, widths, span):
    def portions(a, wanted):
        while depths[a] % (16 * wanted) != 0:
            wanted //= 2
        return wanted

    pieces = [(0, 0, widths[0], 1), (1, 0, widths[1], portions(1, 2))]
    for step in range(widths[2] // span):
        pieces.append((2, step * span, span, portions(2, 4)))
    pieces.append((3, 0, widths[3], portions(3, 4)))
    for a in (4, 5, 6):
        half = widths[a] // 2
        for part in range(2):
            wanted = 2 if (a, part) in ((5, 0), (6, 1)) else 4
            pieces.append((a, part * half, half, portions(a, wanted)))
    return pieces


def forward(tokens, shards, heads, tap_width):
    count = lax.axis_size("fsdp")
    rows, width = tokens.shape
    size = width // heads
    span = GROUP * size
    groups = heads // GROUP
    chunks = rows // CHUNK
    wide_rows = rows + HALO
    depths = [shard.shape[0] for shard in shards]
    widths = [shard.shape[1] for shard in shards]
    pieces = plan_pieces(depths, widths, 3 * span)
    anywhere = pl.BlockSpec(memory_space=pl.ANY)
    shape = jax.ShapeDtypeStruct
    return pl.pallas_call(
        functools.partial(forward_kernel, count, pieces, 2, heads, tap_width),
        grid=(groups,),
        in_specs=[anywhere] * (1 + ARRAYS),
        out_specs=[anywhere] * (ARRAYS + 1)
        + [
            pl.BlockSpec((wide_rows, width), lambda g: (0, 0)),
            pl.BlockSpec((wide_rows, 3 * span), lambda g: (0, g)),
            pl.BlockSpec((rows, widths[1]), lambda g: (0, 0)),
            pl.BlockSpec((GROUP, 3, TAPS, size), lambda g: (g, 0, 0, 0)),
            pl.BlockSpec((rows, span), lambda g: (0, g)),
            pl.BlockSpec((rows, span), lambda g: (0, g)),
            pl.BlockSpec((rows, 2 * span), lambda g: (0, g)),
            pl.BlockSpec((rows, GROUP * CHUNK), lambda g: (0, g)),
            pl.BlockSpec((GROUP, chunks, size, 2 * size), lambda g: (g, 0, 0, 0)),
        ],
        out_shape=[shape((count * d, w), bf16) for d, w in zip(depths, widths)]
        + [
            shape((4, heads, size, 2 * size), bf16),
            shape((wide_rows, width), bf16),
            shape((wide_rows, 3 * width), bf16),
            shape((rows, widths[1]), bf16),
            shape((heads, 3, TAPS, size), f32),
            shape((rows, width), f32),
            shape((rows, width), bf16),
            shape((rows, 2 * width), bf16),
            shape((rows, heads * CHUNK), bf16),
            shape((heads, chunks, size, 2 * size), bf16),
        ],
        scratch_shapes=[
            pltpu.VMEM((wide_rows, width), bf16),
            pltpu.VMEM((1, width, 3 * span), bf16),
            pltpu.VMEM((width, widths[1]), bf16),
            pltpu.VMEM((count * PACK[0], PACK[1]), bf16),
            pltpu.VMEM((TAPS, 3 * width), f32),
            pltpu.VMEM((wide_rows, size), f32),
            pltpu.VMEM((CHUNK.bit_length() - 1, CHUNK, CHUNK), bf16),
            pltpu.VMEM((heads, size, 2 * size), bf16),
            pltpu.SemaphoreType.DMA((2,)),
            pltpu.SemaphoreType.DMA((2,)),
            pltpu.SemaphoreType.DMA((2,)),
            pltpu.SemaphoreType.DMA((2, groups, 4)),
        ]
        + Gather.scratch(pieces, count),
        compiler_params=pltpu.CompilerParams(
            collective_id=0, has_side_effects=True, vmem_limit_bytes=60 * MIB
        ),
    )(tokens, *shards)


def mix_kernel(position_ref, out_ref, carry_ref, finals_ref, gain_ref, mixed_ref, state_ref):
    position = position_ref[0]
    size = out_ref.shape[1]
    state = jnp.zeros((size, size), f32)
    for index in range(finals_ref.shape[0] - 1):
        pair = finals_ref[index, 0].astype(f32)
        later = pair[:, :size] + jnp.dot(pair[:, size:], state, precision=highest)
        state = jnp.where(index < position, later, state)
    state_ref[0] = state
    output = out_ref[...] + nn(carry_ref[...], state.astype(bf16))
    gain = gain_ref[...].astype(f32)
    mixed_ref[...] = rms_scale(output, gain).astype(bf16)


def mix(position, outputs, carries, finals, gain):
    rows, width = outputs.shape
    groups, heads, size, _ = finals.shape
    plain = pl.BlockSpec((rows, size), lambda h: (0, h))
    return pl.pallas_call(
        mix_kernel,
        grid=(heads,),
        in_specs=[
            pl.BlockSpec(memory_space=pltpu.SMEM),
            plain,
            plain,
            pl.BlockSpec((groups, 1, size, 2 * size), lambda h: (0, h, 0, 0)),
            pl.BlockSpec((1, size), lambda h: (0, 0)),
        ],
        out_specs=[plain, pl.BlockSpec((1, size, size), lambda h: (h, 0, 0))],
        out_shape=[
            jax.ShapeDtypeStruct((rows, width), bf16),
            jax.ShapeDtypeStruct((heads, size, size), f32),
        ],
        compiler_params=pltpu.CompilerParams(vmem_limit_bytes=32 * MIB),
    )(position, outputs, carries, finals, gain)


def unmix_kernel(
    out_ref, carry_ref, state_ref, gain_ref, grad_ref, grad_out_ref, grad_state_ref, grad_gain_ref
):
    output = out_ref[...] + nn(carry_ref[...], state_ref[0].astype(bf16))
    gain = gain_ref[...].astype(f32)
    grad = grad_ref[...].astype(f32)
    scaling = lax.rsqrt(jnp.mean(output * output, axis=1, keepdims=True) + epsilon)
    unit_rows = output * scaling

    @pl.when(pl.program_id(0) == 0)
    def _():
        grad_gain_ref[...] = jnp.zeros_like(grad_gain_ref)

    grad_gain_ref[...] += jnp.sum(grad * unit_rows, axis=0, keepdims=True)
    scaled = grad * gain
    grad_out = scaling * (scaled - unit_rows * jnp.mean(scaled * unit_rows, axis=1, keepdims=True))
    low_grad = grad_out.astype(bf16)
    grad_state_ref[0] = tn(carry_ref[...], low_grad)
    grad_out_ref[...] = (grad_out * output.shape[1] ** (-0.5)).astype(bf16)


def unmix(outputs, carries, states, gain, grad_heads):
    rows, width = outputs.shape
    heads, size, _ = states.shape
    plain = pl.BlockSpec((rows, size), lambda h: (0, h))
    state = pl.BlockSpec((1, size, size), lambda h: (h, 0, 0))
    vector = pl.BlockSpec((1, size), lambda h: (0, 0))
    return pl.pallas_call(
        unmix_kernel,
        grid=(heads,),
        in_specs=[plain, plain, state, vector, plain],
        out_specs=[plain, state, vector],
        out_shape=[
            jax.ShapeDtypeStruct((rows, width), bf16),
            jax.ShapeDtypeStruct((heads, size, size), f32),
            jax.ShapeDtypeStruct((1, size), f32),
        ],
        compiler_params=pltpu.CompilerParams(vmem_limit_bytes=32 * MIB),
    )(outputs, carries, states, gain, grad_heads)


def backward_kernel(
    signals_ref,
    logit_ref,
    taps_ref,
    grad_ref,
    fresh_ref,
    inverse_ref,
    starts_ref,
    state_ref,
    grad_state_ref,
    grad_signals_ref,
    tails_ref,
    firsts_ref,
    grad_taps_ref,
    grad_logit_ref,
    wides,
    pres,
    grads,
    padded,
):
    group = pl.program_id(0)
    rows, span = grad_ref.shape
    size = span // BACK
    chunks = rows // CHUNK
    row, col = grid_indices()
    lower, upper = row >= col, row <= col

    def tap_row(which):
        return jnp.concatenate([taps_ref[inner, which] for inner in range(BACK)], axis=1)

    def split(values):
        return [values[:, inner * size : (inner + 1) * size] for inner in range(BACK)]

    lows, scales = [], []
    for which in range(3):
        wides[which] = signals_ref[:, pl.ds(which * span, span)].astype(f32)
        pre = conv_pre(wides.at[which], tap_row(which), rows)
        pres[which] = pre
        act = split(pre * sigmoid(pre))
        if which < 2:
            scale = [
                lax.rsqrt(jnp.sum(part * part, axis=1, keepdims=True) + epsilon) for part in act
            ]
            act = [part * one for part, one in zip(act, scale)]
            scales.append(scale)
        lows.append([part.astype(bf16) for part in act])
    queries, keys, values = lows
    logits = logit_ref[...].astype(f32)
    rates = [sigmoid(head_column(logits, group * BACK + inner)) for inner in range(BACK)]

    states = [state_ref[inner].astype(bf16) for inner in range(BACK)]
    fresh_all = []
    for inner in range(BACK):
        first = fresh_ref[:, pl.ds(inner * 2 * size, size)].astype(f32)
        second = fresh_ref[:, pl.ds((inner * 2 + 1) * size, size)]
        fresh_all.append((first + nn(second, states[inner])).astype(bf16))

    grad_memories = [grad_state_ref[inner] for inner in range(BACK)]
    grad_rates = [[None] * chunks for _ in range(BACK)]
    for chunk in reversed(range(chunks)):
        part = slice(chunk * CHUNK, (chunk + 1) * CHUNK)
        for inner in range(BACK):
            key, query, value = keys[inner][part], queries[inner][part], values[inner][part]
            rate = rates[inner][part]
            columns = slice(inner * size, (inner + 1) * size)
            grad_out = grad_ref[part, columns]
            fresh = fresh_all[inner][part]
            start = starts_ref[inner, chunk]
            memory = (start[:, :size].astype(f32) + nn(start[:, size:], states[inner])).astype(
                bf16
            )
            low_grad = grad_memories[inner].astype(bf16)
            key_f = key.astype(f32)
            rated = (rate * key_f).astype(bf16)

            scores_t = jnp.where(upper, nt(key, query), 0.0).astype(bf16)
            grad_fresh = (nn(scores_t, grad_out) + nn(key, low_grad)).astype(bf16)
            aim = tn(inverse_ref[part, inner * CHUNK : (inner + 1) * CHUNK], grad_fresh)
            low_aim = aim.astype(bf16)
            grad_memories[inner] = (
                grad_memories[inner] + tn(query, grad_out) - tn(rated, low_aim)
            )

            grad_scores = jnp.where(lower, nt(grad_out, fresh), 0.0).astype(bf16)
            grad_scores_t = jnp.where(upper, nt(fresh, grad_out), 0.0).astype(bf16)
            grad_strict = jnp.where(row > col, nt(low_aim, fresh), 0.0).astype(bf16)
            grad_strict_t = jnp.where(row < col, nt(fresh, low_aim), 0.0).astype(bf16)

            grad_query = nt(grad_out, memory) + nn(grad_scores, key)
            within = -(nn(grad_strict, key) + nt(low_aim, memory))
            grad_rates[inner][chunk] = jnp.sum(
                key_f * within + value.astype(f32) * aim, axis=1, keepdims=True
            )
            grad_key = (
                rate * within
                - nn(grad_strict_t, rated)
                + nn(grad_scores_t, query)
                + nt(fresh, low_grad)
            )
            grads[0, part, columns] = grad_query
            grads[1, part, columns] = grad_key
            grads[2, part, columns] = rate * aim

    @pl.when(group == 0)
    def _():
        grad_logit_ref[...] = jnp.zeros_like(grad_logit_ref)
        padded[...] = jnp.zeros_like(padded)

    lane = lax.broadcasted_iota(jnp.int32, grad_logit_ref.shape, 1)
    for inner in range(BACK):
        grad_rate = jnp.concatenate(grad_rates[inner], axis=0)
        grad_logit = grad_rate * rates[inner] * (1.0 - rates[inner])
        grad_logit_ref[...] = jnp.where(
            lane == group * BACK + inner, grad_logit, grad_logit_ref[...]
        )

    for which in range(3):
        taps = tap_row(which)
        pre = pres[which]
        sig = sigmoid(pre)
        grad_act = grads[which]
        if which < 2:
            unit_rows = split(pre * sig)
            parts = []
            for one, unit, scale in zip(split(grad_act), unit_rows, scales[which]):
                unit = unit * scale
                parts.append(scale * (one - unit * jnp.sum(one * unit, axis=1, keepdims=True)))
            grad_act = jnp.concatenate(parts, axis=1)
        grad_pre = grad_act * sig * (1.0 + pre * (1.0 - sig))
        padded[pl.ds(HALO, rows), :] = grad_pre
        for offset in range(TAPS):
            shifted = wides[which, pl.ds(HALO - TAPS + 1 + offset, rows), :]
            total = jnp.sum(grad_pre * shifted, axis=0, keepdims=True)
            for inner, one in enumerate(split(total)):
                grad_taps_ref[inner, which, pl.ds(offset, 1), :] = one

        def back(start, number):
            total = None
            for offset in range(TAPS):
                term = (
                    taps[offset : offset + 1, :]
                    * padded[pl.ds(start + TAPS - 1 - offset, number), :]
                )
                total = term if total is None else total + term
            return total

        columns = pl.ds(which * span, span)
        grad_signal = back(HALO, rows)
        grad_signals_ref[:, columns] = grad_signal.astype(bf16)
        tails_ref[:, columns] = grad_signal[rows - HALO :]
        firsts_ref[:, columns] = back(0, HALO)


def delta_backward(
    signals, logits, taps, grad_out, fresh, inverses, starts, state, grad_state
):
    wide_rows = signals.shape[0]
    rows, width = grad_out.shape
    heads, _, _, size = taps.shape
    span = BACK * size
    chunks = rows // CHUNK
    whole = pl.BlockSpec(logits.shape, lambda g: (0, 0))
    tap = pl.BlockSpec((BACK, 3, TAPS, size), lambda g: (g, 0, 0, 0))
    state_spec = pl.BlockSpec((BACK, size, size), lambda g: (g, 0, 0))
    edge = pl.BlockSpec((HALO, 3 * span), lambda g: (0, g))
    return pl.pallas_call(
        backward_kernel,
        grid=(heads // BACK,),
        in_specs=[
            pl.BlockSpec((wide_rows, 3 * span), lambda g: (0, g)),
            whole,
            tap,
            pl.BlockSpec((rows, span), lambda g: (0, g)),
            pl.BlockSpec((rows, 2 * span), lambda g: (0, g)),
            pl.BlockSpec((rows, BACK * CHUNK), lambda g: (0, g)),
            pl.BlockSpec((BACK, chunks, size, 2 * size), lambda g: (g, 0, 0, 0)),
            state_spec,
            state_spec,
        ],
        out_specs=[pl.BlockSpec((rows, 3 * span), lambda g: (0, g)), edge, edge, tap, whole],
        out_shape=[
            jax.ShapeDtypeStruct((rows, 3 * width), bf16),
            jax.ShapeDtypeStruct((HALO, 3 * width), f32),
            jax.ShapeDtypeStruct((HALO, 3 * width), f32),
            jax.ShapeDtypeStruct(taps.shape, f32),
            jax.ShapeDtypeStruct(logits.shape, f32),
        ],
        scratch_shapes=[
            pltpu.VMEM((3, wide_rows, span), f32),
            pltpu.VMEM((3, rows, span), f32),
            pltpu.VMEM((3, rows, span), f32),
            pltpu.VMEM((rows + 2 * HALO, span), f32),
        ],
        compiler_params=pltpu.CompilerParams(vmem_limit_bytes=60 * MIB),
    )(signals, logits, taps, grad_out, fresh, inverses, starts, state, grad_state)


def batched(left_side, right_side, transpose_left=False):
    return lax.dot_general(
        left_side,
        right_side,
        (((1 if transpose_left else 2,), (1,)), ((0,), (0,))),
        precision=highest,
        preferred_element_type=f32,
    )


def local(
    inputs,
    g_attn,
    w_query,
    w_key,
    w_value,
    w_beta,
    conv_taps,
    o_gain,
    w_out,
    g_mlp,
    w_gate,
    w_up,
    w_down,
    cotangent,
):
    count = lax.axis_size("fsdp")
    position = lax.axis_index("seq")
    groups = lax.axis_size("seq")
    tokens_low = inputs[0]
    rows, width = tokens_low.shape
    heads = w_beta.shape[1]
    size = width // heads
    depth = w_query.shape[0]
    small = (g_attn.shape, g_mlp.shape, o_gain.shape, conv_taps.shape)
    packed = pack_small((g_attn[None], g_mlp[None], o_gain[None]), conv_taps[None])
    mixed = jnp.stack([w.reshape(depth, -1, size) for w in (w_query, w_key, w_value)], axis=2)
    shards = (
        packed,
        jnp.pad(w_beta, ((0, 0), (0, 128 - heads))),
        mixed.reshape(depth, 3 * width),
        w_out,
        w_gate,
        w_up,
        jnp.transpose(w_down),
    )
    results = forward(tokens_low, shards, heads, conv_taps.shape[1])
    packed, w_beta, w_mixed, w_out, w_gate, w_up, w_down_t = results[:ARRAYS]
    finals, wide_normed, signals, logits, taps = results[ARRAYS : ARRAYS + 5]
    outputs, carries, fresh, inverses, starts = results[ARRAYS + 5 :]
    g_attn, g_mlp, o_gain, _ = unpack_small(packed, small)
    g_attn, g_mlp, o_gain = g_attn.reshape(-1), g_mlp.reshape(-1), o_gain.reshape(-1)
    gain_attn = g_attn.astype(f32)
    tokens = tokens_low.astype(f32)
    normed = wide_normed[HALO:]

    gain_out = o_gain.reshape(1, size)
    head_rows, state_in = mix(position.reshape(1), outputs, carries, finals, gain_out)
    attended = tokens + nn(head_rows, w_out)
    gain_mlp = g_mlp.astype(f32)
    normed_ff = rms_scale(attended, gain_mlp).astype(bf16)
    gated = nn(normed_ff, w_gate)
    upward = nn(normed_ff, w_up)
    sigmoid_gate = jax.nn.sigmoid(gated)
    activated = gated * sigmoid_gate
    hidden = (activated * upward).astype(bf16)
    layer_out = (attended + nt(hidden, w_down_t)).astype(bf16)

    grad_out = cotangent[0]
    grad_down_t = tn(grad_out, hidden).astype(bf16)
    grad_hidden = nn(grad_out, w_down_t)
    grad_gate = (grad_hidden * upward * sigmoid_gate * (1.0 + gated * (1.0 - sigmoid_gate))).astype(
        bf16
    )
    grad_upward = (grad_hidden * activated).astype(bf16)
    grad_gate_matrix = tn(normed_ff, grad_gate).astype(bf16)
    grad_up_matrix = tn(normed_ff, grad_upward).astype(bf16)
    grad_normed_ff = nt(grad_gate, w_gate) + nt(grad_upward, w_up)
    grad_from_ff, grad_gain_mlp = norm_backward(attended, gain_mlp, grad_normed_ff)
    grad_attended = grad_out.astype(f32) + grad_from_ff

    grad_mixed = grad_attended.astype(bf16)
    grad_out_matrix = tn(head_rows, grad_mixed).astype(bf16)
    grad_heads = nt(grad_mixed, w_out).astype(bf16)
    grad_delta, grad_starts, grad_gain_out = unmix(
        outputs, carries, state_in, gain_out, grad_heads
    )
    grads_all = lax.all_gather(grad_starts, "seq", axis=0)
    grad_state = jnp.zeros((heads, size, size), f32)
    grad_states = [grad_state]
    for index in reversed(range(1, groups)):
        grad_state = grads_all[index] + batched(
            finals[index, :, :, size:].astype(f32), grad_state, transpose_left=True
        )
        grad_states.append(grad_state)
    grad_states.reverse()
    grad_final = lax.dynamic_index_in_dim(jnp.stack(grad_states), position, 0, keepdims=False)

    grad_signals, tails, firsts, grad_taps, grad_logits = delta_backward(
        signals,
        logits,
        taps,
        grad_delta,
        fresh,
        inverses,
        starts,
        state_in,
        grad_final,
    )
    backward_pairs = [(index + 1, index) for index in range(groups - 1)]
    received = lax.ppermute(firsts, "seq", backward_pairs)
    fixed = (tails + received).astype(bf16)
    grad_signals = lax.dynamic_update_slice(grad_signals, fixed, (rows - HALO, 0))
    grad_logits = grad_logits.astype(bf16)

    grad_mixed_matrix = tn(normed, grad_signals).astype(bf16)
    grad_beta_matrix = jnp.pad(tn(normed, grad_logits).astype(bf16), ((0, 0), (0, 128)))
    grad_normed = nt(grad_signals, w_mixed) + nt(grad_logits, w_beta)
    grad_from_attn, grad_gain_attn = norm_backward(tokens, gain_attn, grad_normed)
    grad_inputs = (grad_attended + grad_from_attn)[None]
    grad_taps = jnp.transpose(grad_taps, (2, 1, 0, 3)).reshape(TAPS, count, -1)
    packed = pack_small(
        [g.reshape(count, -1) for g in (grad_gain_attn, grad_gain_mlp, grad_gain_out)],
        jnp.transpose(grad_taps, (1, 0, 2)),
    )
    grad_gate_matrix, grad_up_matrix, grad_down_t, grad_out_matrix = reduce_all(
        (grad_gate_matrix, grad_up_matrix, grad_down_t, grad_out_matrix), 2
    )
    packed, grad_beta_matrix, grad_mixed_matrix = reduce_all(
        (packed, grad_beta_matrix, grad_mixed_matrix), 3
    )
    parts = [part[0].astype(f32) for part in unpack_small(packed, small)]
    grad_gain_attn, grad_gain_mlp, grad_gain_out, grad_taps = parts
    grad_mixed_matrix = grad_mixed_matrix.astype(f32).reshape(depth, heads, 3, size)
    grad_query_matrix, grad_key_matrix, grad_value_matrix = (
        grad_mixed_matrix[:, :, which].reshape(depth, width) for which in range(3)
    )
    return (
        layer_out[None],
        grad_inputs,
        grad_gain_attn,
        grad_query_matrix,
        grad_key_matrix,
        grad_value_matrix,
        grad_beta_matrix[:, :heads].astype(f32),
        grad_taps,
        grad_gain_out,
        grad_out_matrix.astype(f32),
        grad_gain_mlp,
        grad_gate_matrix.astype(f32),
        grad_up_matrix.astype(f32),
        jnp.transpose(grad_down_t).astype(f32),
    )


def solution(mesh):
    vector = P("fsdp")
    rows = P("fsdp", None)
    columns = P(None, "fsdp")
    tokens = P("fsdp", "seq", None)
    return jax.shard_map(
        local,
        mesh=mesh,
        in_specs=(
            tokens,
            vector,
            rows,
            rows,
            rows,
            rows,
            columns,
            vector,
            rows,
            vector,
            rows,
            rows,
            columns,
            tokens,
        ),
        out_specs=(
            tokens,
            tokens,
            vector,
            rows,
            rows,
            rows,
            rows,
            columns,
            vector,
            rows,
            vector,
            rows,
            rows,
            columns,
        ),
        check_vma=False,
    )
```

time: 732 us -> 624 us (0.85)
  Pallas kernels: 479 us -> 403 us
  matrix products: 160 us -> 138 us
    pallas_call x5 -> x3, Pallas kernels: 283 us -> 207 us  [the longest x1 146 us: forward(): pl.pallas_call(functools.partial(forward_kernel, count, pieces, 2, heads,...]
    dot_general x8 -> x4, matrix products: 55.3 us -> 41.9 us  [nn(): lax.dot_general(left_side, right_side, (((1,), (0,)), ((), ())), preferre...]
    dot_general x6 -> x3, matrix products: 12.3 us -> 4.68 us  [batched(): lax.dot_general(left_side, right_side, (((1 if transpose_left else 2,), (...]
    unnamed x128 -> x98, local copies, waits for them, and re-layouts: 28.3 us -> 22.2 us
    dot_general x8 -> x6, matrix products: 46 us -> 42.7 us  [nt(): lax.dot_general(left_side, right_side, (((1,), (1,)), ((), ())), preferre...]
    dot_general x8 -> x6, matrix products: 46.8 us -> 48.4 us  [tn(): lax.dot_general(left_side, right_side, (((0,), (0,)), ((), ())), preferre...]
  transfers between devices with their start and end apart: 4 -> 2, of which waited for: 0 -> 0; matrix products, arithmetic and copies ran while one was open for 6% -> 10% of each run, Pallas kernels for 42% -> 21%
where the time goes in v2:
time: 624 us; the launch traced here: 612 us
  Pallas kernels  403 us (65%)
  matrix products  138 us (22%)
  local copies, waits for them, and re-layouts  31.4 us (5%)
  other arithmetic  23.1 us (4%)
  between operations  15 us (2%)
    pallas_call x2, Pallas kernels, reduce_all(): pl.pallas_call(functools.partial(reduce_kernel, arrays, count, pieces), i...  187 us
    pallas_call x1, Pallas kernels, forward(): pl.pallas_call(functools.partial(forward_kernel, count, pieces, 2, heads,...  146 us
    pallas_call x1, Pallas kernels, delta_backward(): pl.pallas_call(backward_kernel, grid=(heads // BACK,), in_specs=[pl.Block...  51.1 us
    dot_general x6, matrix products, tn(): lax.dot_general(left_side, right_side, (((0,), (0,)), ((), ())), preferre...  48.4 us
    dot_general x6, matrix products, nt(): lax.dot_general(left_side, right_side, (((1,), (1,)), ((), ())), preferre...  42.7 us
    dot_general x4, matrix products, nn(): lax.dot_general(left_side, right_side, (((1,), (0,)), ((), ())), preferre...  41.9 us
    unnamed x98, local copies, waits for them, and re-layouts  22.2 us
  transfers between devices with their start and end apart: 2, of which 0 were waited for; matrix products, arithmetic and copies ran while one was open for 10% of the time, Pallas kernels for 21%

profile of v2, /device:TPU:0, one launch (start us, length us, event | category | flops | bytes accessed | tf_op | source)
XLA Modules:
  0.0 612.1 jit_solution(584185342833000317)
XLA Ops:
  7.3 1.2 copy.66
  10.8 1.2 copy.70.refs_3_
  12.0 1.1 copy.69
  14.5 145.7 %shard_map.245 = (bf16[128,512]{1,0:T(8,128)(2,1)}, bf16[1024,128]{1,0:T(8,128)(2,1)}, bf16[1024,3072]{1,0:T(8,128)(2,1)}, bf16[1024,1024]{1,0:T(8,128)(2,1)}, b...) custom-call(bf16[1024,1024]{1,0:T(8,128)(2,1)} %bitcast.134, ...), custom_call_target="tpu_custom_call" | custom-call | tf_op jit(solution)/shard_map/pallas_call | solution.py:972
  160.9 1.4 slice_convert_fusion.1
  162.4 2.2 copy-done
  164.6 1.6 copy-done.2
  166.2 1.6 copy-done.4
  167.8 9.9 %shard_map.246 = (bf16[1024,1024]{1,0:T(8,128)(2,1)S(1)}, f32[8,128,128]{2,1,0:T(8,128)S(1)}) custom-call(s32[1]{0:T(128)} %bitcast.1.position_ref, f32[1024,1024]{1,0:T(8,128)S(1)} %copy-done, bf16[1024,1024]{1,0:T(8,128)(2,1)S(1)} %copy-done.2, bf16[4,8,128,256]{3,2,1,0:T(8,128)(2,1)S(1)} %copy-done.4, bf16[1,128]{1,0:T(2,128)(2,1)S(1)} %reshape_reshape_squeeze.3.gain_ref), custom_call_target="tpu_custom_call" | custom-call | tf_op jit(solution)/shard_map/pallas_call | solution.py:1040
  177.8 2.5 multiply_reduce_fusion.2
  180.3 2.0 copy-done.9
  182.7 8.8 %fusion.69 = f32[1024,2816]{1,0:T(8,128)} fusion(bf16[1024,1024]{1,0:T(8,128)(2,1)S(1)} %multiply_convert_fusion.1, bf16[1024,2816]{1,0:T(8,128)(2,1)S(1)} %bitcast.172), kind=kOutput, calls=%fused_computation.126 | convolution fusion | flops 5905580032 | bytes 19398656 | tf_op jit(solution)/shard_map/dot_general | solution.py:22
  191.6 8.8 %fusion.68 = f32[1024,2816]{1,0:T(8,128)} fusion(bf16[1024,1024]{1,0:T(8,128)(2,1)S(1)} %multiply_convert_fusion.1, bf16[1024,2816]{1,0:T(8,128)(2,1)S(1)} %bitcast.174), kind=kOutput, calls=%fused_computation.125 | convolution fusion | flops 5905580032 | bytes 19398656 | tf_op jit(solution)/shard_map/dot_general | solution.py:22
  200.4 21.8 %fusion.3 = (bf16[1024,2816]{1,0:T(8,128)(2,1)}, bf16[1024,2816]{1,0:T(8,128)(2,1)}, bf16[1024,2816]{1,0:T(8,128)(2,1)}) fusion(f32[1024,2816]{1,0:T(8,128)} %fusion.68, f32[1024,2816]{1,0:T(8,128)} %fusion.69, bf16[1024,2816]{1,0:T(8,128)(2,1)} %get-tuple-element.56, bf16[1,1024,1024]{2,1,0:T(8,128)(2,1)} %param.27), kind=kOutput, calls=%fused_computation.5 | convolution fusion | flops 5948833792 | bytes 48234496 | tf_op jit(solution)/shard_map/dot_general | solution.py:22
  222.2 10.0 %fusion.70 = f32[1024,1024]{1,0:T(8,128)S(1)} fusion(bf16[1024,2816]{1,0:T(8,128)(2,1)} %get-tuple-element.129, bf16[1024,2816]{1,0:T(8,128)(2,1)} %get-tuple-element.54), kind=kOutput, calls=%fused_computation.127 | convolution fusion | flops 5905580032 | bytes 15728640 | tf_op jit(solution)/shard_map/dot_general | solution.py:28
  232.3 9.1 %multiply_reduce_fusion = (bf16[1024]{0:T(1024)(128)(2,1)S(1)}, f32[1024]{0:T(1024)S(1)}, f32[1024,1024]{1,0:T(8,128)S(1)}) fusion(f32[1024,1024]{1,0:T(8,128)S(1)} %copy-done.10, f32[1024]{0:T(1024)S(1)} %add_rsqrt_fusion.1, f32[1024]{0:T(1024)S(1)} %bitcast.154, f32[1024,1024]{1,0:T(8,128)S(1)} %fusion.70, bf16[1024,2816]{1,0:T(8,128)(2,1)S(1)} %copy-done.33, ...), kind=kOutput, calls=%fused_computation.26 | convolution fusion | flops 5912918016 | bytes 24131584 | tf_op jit(solution)/shard_map/dot_general | solution.py:28
  241.4 1.3 multiply_add_fusion
  243.0 2.4 convolution_convert_fusion.5.grad_ref
  245.5 1.3 copy-done.1
  247.4 9.6 %shard_map.247 = (bf16[1024,1024]{1,0:T(8,128)(2,1)S(1)}, f32[8,128,128]{2,1,0:T(8,128)}, f32[1,128]{1,0:T(1,128)S(1)}) custom-call(f32[1024,1024]{1,0:T(8,128)S(1)} %copy-done.1, bf16[1024,1024]{1,0:T(8,128)(2,1)S(1)} %copy-done.3, f32[8,128,128]{2,1,0:T(8,128)S(1)} %get-tuple-element.60.state_ref, bf16[1,128]{1,0:T(2,128)(2,1)S(1)} %reshape_reshape_squeeze.3.gain_ref, ...), custom_call_target="tpu_custom_call" | custom-call | tf_op jit(solution)/shard_map/pallas_call | solution.py:1086
  257.0 1.4 copy-done.5
  258.5 6.1 convolution_convert_fusion.4
  264.6 10.8 %convolution_convert_fusion.1 = bf16[1024,2816]{1,0:T(8,128)(2,1)} fusion(bf16[1024,1024]{1,0:T(8,128)(2,1)S(1)} %copy-done.13, bf16[1024,2816]{1,0:T(8,128)(2,1)} %get-tuple-element.128), kind=kOutput, calls=%fused_computation.16 | convolution fusion | flops 5908463616 | bytes 13631488 | tf_op jit(solution)/shard_map/dot_general | solution.py:34
  275.5 8.4 %convolution_convert_fusion.2 = bf16[1024,2816]{1,0:T(8,128)(2,1)} fusion(bf16[1024,1024]{1,0:T(8,128)(2,1)S(1)} %copy-done.13, bf16[1024,2816]{1,0:T(8,128)(2,1)S(1)} %bitcast.176), kind=kOutput, calls=%fused_computation.17 | convolution fusion | flops 5908463616 | bytes 13631488 | tf_op jit(solution)/shard_map/dot_general | solution.py:34
  283.8 8.4 %convolution_convert_fusion = bf16[2816,1024]{0,1:T(8,128)(2,1)} fusion(bf16[1024,2816]{1,0:T(8,128)(2,1)S(1)} %bitcast.178, bf16[1,1024,1024]{2,1,0:T(8,128)(2,1)S(1)} %copy-done.15), kind=kOutput, calls=%fused_computation.15 | convolution fusion | flops 5908463616 | bytes 13631488 | tf_op jit(solution)/shard_map/dot_general | solution.py:34
  292.3 127.1 %shard_map.250 = (bf16[128,2816]{1,0:T(8,128)(2,1)}, bf16[128,2816]{1,0:T(8,128)(2,1)}, bf16[128,2816]{1,0:T(8,128)(2,1)}, bf16[128,1024]{1,0:T(8,128)(2,1)}) custom-call(bf16[8,128,2816]{2,1,0:T(8,128)(2,1)} %bitcast.138, bf16[8,128,2816]{2,1,0:T(8,128)(2,1)} %bitcast.137, bf16[8,128,2816]{2,1,0:T(8,128)(2,1)} %bitcast.139, bf16[8,128,1024]{2,1,0:T(8,128)(2,1)} %bitcast.144), custom_call_target="tpu_custom_call" | custom-call | tf_op jit(solution)/shard_map/pallas_call | solution.py:372
  419.4 1.2 convert_bitcast_fusion
  420.6 1.5 copy.87
  422.2 2.3 convert_element_type.234
  424.5 2.3 convert_element_type.235
  428.9 11.5 %fusion.15 = bf16[1,1024,1024]{2,1,0:T(8,128)(2,1)} fusion(f32[1024,1024]{1,0:T(8,128)} %copy-done.9, bf16[1024,2816]{1,0:T(8,128)(2,1)} %get-tuple-element.130, bf16[1024,2816]{1,0:T(8,128)(2,1)} %get-tuple-element.56), kind=kOutput, calls=%fused_computation.32 | convolution fusion | flops 5907677184 | bytes 17825792 | tf_op jit(solution)/shard_map/dot_general | solution.py:28
  440.4 1.5 convolution_add_fusion.4
  442.0 1.6 convolution_add_fusion.3
  443.6 1.6 fusion.22
  445.1 1.6 fusion.31.grad_state_ref
  446.7 51.1 %shard_map.248 = (bf16[1024,3072]{1,0:T(8,128)(2,1)}, f32[16,3072]{1,0:T(8,128)}, f32[16,3072]{1,0:T(8,128)}, f32[8,3,4,128]{3,2,1,0:T(4,128)}, f32[1024,128]{1,0:T(8,128)}) custom-call(bf16[1040,3072]{1,0:T(8,128)(2,1)} %get-tuple-element.57.signals_ref, bf16[1024,128]{1,0:T(8,128)(2,1)} %get-tuple-element.58.logit_ref, ...), custom_call_target="tpu_custom_call" | custom-call | tf_op jit(solution)/shard_map/pallas_call | solution.py:1265
  497.9 1.4 collective-permute-start
  499.3 2.5 fusion.23
  504.3 12.2 %convolution_convert_fusion.3 = bf16[1024,3072]{1,0:T(8,128)(2,1)} fusion(bf16[1024,3072]{1,0:T(8,128)(2,1)} %fusion.51, bf16[1040,1024]{1,0:T(8,128)(2,1)S(1)} %copy-done.30), kind=kOutput, calls=%fused_computation.18 | convolution fusion | flops 6445596672 | bytes 14680064 | tf_op jit(solution)/shard_map/dot_general | solution.py:34
  516.5 9.0 %fusion.13 = (bf16[1024]{0:T(1024)(128)(2,1)S(1)}, f32[1024]{0:T(1024)S(1)}, f32[1024,1024]{1,0:T(8,128)}) fusion(f32[1024]{0:T(1024)S(1)} %add_rsqrt_fusion, bf16[1,1024,1024]{2,1,0:T(8,128)(2,1)S(1)} %copy-done.8, f32[1024]{0:T(1024)S(1)} %bitcast.156, f32[1024,1024]{1,0:T(8,128)S(1)} %fusion.49, bf16[1024,3072]{1,0:T(8,128)(2,1)S(1)} %copy-done.29, ...), kind=kOutput, calls=%fused_computation.24 | convolution fusion | flops 6450837504 | bytes 23083008 | tf_op jit(solution)/shard_map/dot_general | solution.py:28
  526.2 59.9 %shard_map.249 = (bf16[16,512]{1,0:T(8,128)(2,1)}, bf16[128,256]{1,0:T(8,128)(2,1)}, bf16[128,3072]{1,0:T(8,128)(2,1)}) custom-call(bf16[8,16,512]{2,1,0:T(8,128)(2,1)} %fusion.46.refs_0_, bf16[8,128,256]{2,1,0:T(8,128)(2,1)} %bitcast.148, bf16[8,128,3072]{2,1,0:T(8,128)(2,1)} %bitcast.136), custom_call_target="tpu_custom_call" | custom-call | tf_op jit(solution)/shard_map/pallas_call | solution.py:372
  586.1 1.3 fusion.62
  587.4 1.3 fusion.63
  588.7 1.2 fusion.64
  589.9 2.6 copy.82
  592.5 2.3 fusion.67
  594.8 2.0 copy.83
  599.5 5.4 fusion.12
  (124 shorter events, 14.0 us)
Async XLA Ops:
  7.2 4.8 copy-start.16
  7.2 5.9 copy-start.25
  7.2 6.7 %copy-start.28 = (bf16[128]{0:T(256)(128)(2,1)S(1)}, bf16[128]{0:T(256)(128)(2,1)}, u32[]{:S(2)}) copy-start(bf16[128]{0:T(256)(128)(2,1)} %param.15) | copy-start | bytes 772
  7.2 6.7 %copy-start.27 = (bf16[128]{0:T(256)(128)(2,1)S(1)}, bf16[128]{0:T(256)(128)(2,1)}, u32[]{:S(2)}) copy-start(bf16[128]{0:T(256)(128)(2,1)} %param.23) | copy-start | bytes 772
  7.2 6.7 %copy-start.26 = (bf16[16]{0:T(256)(128)(2,1)S(1)}, bf16[16]{0:T(256)(128)(2,1)}, u32[]{:S(2)}) copy-start(bf16[16]{0:T(256)(128)(2,1)} %param.21) | copy-start | bytes 100
  7.2 6.7 %copy-start.24 = (bf16[4,384]{1,0:T(4,128)(2,1)S(1)}, bf16[4,384]{1,0:T(4,128)(2,1)}, u32[]{:S(2)}) copy-start(bf16[4,384]{1,0:T(4,128)(2,1)} %param.20) | copy-start | bytes 9220
  7.2 433.2 %all-gather.3.cloned.1.call-start = ((), (), s32[]{:S(2)}) async-start(), calls=%async_computation | async-start | bytes 2621440 | tf_op jit(solution)/shard_map/all_gather | solution.py:1384
  162.4 2.2 copy-start
  164.6 1.6 copy-start.2
  166.2 1.6 copy-start.4
  167.8 10.0 %copy-start.7 = (bf16[1,1024,1024]{2,1,0:T(8,128)(2,1)S(1)}, bf16[1,1024,1024]{2,1,0:T(8,128)(2,1)}, u32[]{:S(2)}) copy-start(bf16[1,1024,1024]{2,1,0:T(8,128)(2,1)} %param.14) | copy-start | bytes 6291460
  167.8 10.0 %copy-start.31 = (bf16[1024,1024]{1,0:T(8,128)(2,1)S(1)}, bf16[1024,1024]{1,0:T(8,128)(2,1)}, u32[]{:S(2)}) copy-start(bf16[1024,1024]{1,0:T(8,128)(2,1)} %get-tuple-element.53) | copy-start | bytes 6291460
  177.7 67.7 %copy-start.6 = (f32[8,128,128]{2,1,0:T(8,128)}, f32[8,128,128]{2,1,0:T(8,128)S(1)}, u32[]{:S(2)}) copy-start(f32[8,128,128]{2,1,0:T(8,128)S(1)} %get-tuple-element.60.state_ref) | copy-start | bytes 1572868
  177.7 5.0 slice-start.2
  177.8 4.9 slice-start.3
  180.2 2.0 copy-start.9
  182.3 9.3 %slice-start.4 = ((s8[5767168]{0:T(1024)(128)(4,1)}), s8[4194304]{0:T(1024)(128)(4,1)S(1)}, s32[]{:S(2)}) async-start(s8[5767168]{0:T(1024)(128)(4,1)} %bitcast.173), calls=%async_computation.5 | async-start | bytes 8388608
  182.7 8.9 %copy-start.12 = (bf16[1024,1024]{1,0:T(8,128)(2,1)}, bf16[1024,1024]{1,0:T(8,128)(2,1)S(1)}, u32[]{:S(2)}) copy-start(bf16[1024,1024]{1,0:T(8,128)(2,1)S(1)} %multiply_convert_fusion.1) | copy-start | bytes 6291460
  182.7 8.9 %slice-start.5 = ((s8[5767168]{0:T(1024)(128)(4,1)}), s8[1572864]{0:T(1024)(128)(4,1)S(1)}, s32[]{:S(2)}) async-start(s8[5767168]{0:T(1024)(128)(4,1)} %bitcast.173), calls=%async_computation.6 | async-start | bytes 3145728
  222.2 10.0 %copy-start.10 = (f32[1024,1024]{1,0:T(8,128)S(1)}, f32[1024,1024]{1,0:T(8,128)}, u32[]{:S(2)}) copy-start(f32[1024,1024]{1,0:T(8,128)} %copy-done.9) | copy-start | bytes 12582916
  222.2 10.0 %copy-start.33 = (bf16[1024,2816]{1,0:T(8,128)(2,1)S(1)}, bf16[1024,2816]{1,0:T(8,128)(2,1)}, u32[]{:S(2)}) copy-start(bf16[1024,2816]{1,0:T(8,128)(2,1)} %get-tuple-element.128) | copy-start | bytes 17301508
  232.3 9.1 %copy-start.14 = (bf16[1,1024,1024]{2,1,0:T(8,128)(2,1)S(1)}, bf16[1,1024,1024]{2,1,0:T(8,128)(2,1)}, u32[]{:S(2)}) copy-start(bf16[1,1024,1024]{2,1,0:T(8,128)(2,1)} %param.27) | copy-start | bytes 6291460
  241.4 1.6 copy-start.32
  243.0 2.4 copy-start.11
  243.0 3.7 copy-start.1
  243.0 4.4 copy-start.3
  257.0 1.4 copy-start.5
  258.5 6.1 %copy-start.13 = (bf16[1024,1024]{1,0:T(8,128)(2,1)S(1)}, bf16[1024,1024]{1,0:T(8,128)(2,1)}, u32[]{:S(2)}) copy-start(bf16[1024,1024]{1,0:T(8,128)(2,1)} %copy-done.12) | copy-start | bytes 6291460
  258.5 17.0 %slice-start.6 = ((s8[5767168]{0:T(1024)(128)(4,1)}), s8[4194304]{0:T(1024)(128)(4,1)S(1)}, s32[]{:S(2)}) async-start(s8[5767168]{0:T(1024)(128)(4,1)} %bitcast.175), calls=%async_computation.7 | async-start | bytes 8388608
  264.6 10.9 %slice-start.7 = ((s8[5767168]{0:T(1024)(128)(4,1)}), s8[1572864]{0:T(1024)(128)(4,1)S(1)}, s32[]{:S(2)}) async-start(s8[5767168]{0:T(1024)(128)(4,1)} %bitcast.175), calls=%async_computation.8 | async-start | bytes 3145728
  264.6 19.2 %slice-start.8 = ((s8[5767168]{0:T(1024)(128)(4,1)}), s8[4194304]{0:T(1024)(128)(4,1)S(1)}, s32[]{:S(2)}) async-start(s8[5767168]{0:T(1024)(128)(4,1)} %bitcast.177), calls=%async_computation.9 | async-start | bytes 8388608
  275.4 8.4 %copy-start.15 = (bf16[1,1024,1024]{2,1,0:T(8,128)(2,1)S(1)}, bf16[1,1024,1024]{2,1,0:T(8,128)(2,1)}, u32[]{:S(2)}) copy-start(bf16[1,1024,1024]{2,1,0:T(8,128)(2,1)} %param.27) | copy-start | bytes 6291460
  275.5 8.4 %slice-start.9 = ((s8[5767168]{0:T(1024)(128)(4,1)}), s8[1572864]{0:T(1024)(128)(4,1)S(1)}, s32[]{:S(2)}) async-start(s8[5767168]{0:T(1024)(128)(4,1)} %bitcast.177), calls=%async_computation.10 | async-start | bytes 3145728
  420.6 7.8 %copy-start.8 = (bf16[1,1024,1024]{2,1,0:T(8,128)(2,1)S(1)}, bf16[1,1024,1024]{2,1,0:T(8,128)(2,1)}, u32[]{:S(2)}) copy-start(bf16[1,1024,1024]{2,1,0:T(8,128)(2,1)} %param.14) | copy-start | bytes 6291460
  422.2 4.7 copy-start.19
  497.9 4.8 copy-start.21
  497.9 4.9 copy-start.17
  497.9 4.9 copy-start.18
  497.9 5.6 collective-permute-start
  499.3 4.2 copy-start.20
  502.7 1.6 copy-start.30
  502.8 13.7 %slice-start = ((s8[6291456]{0:T(1024)(128)(4,1)}), s8[4194304]{0:T(1024)(128)(4,1)S(1)}, s32[]{:S(2)}) async-start(s8[6291456]{0:T(1024)(128)(4,1)} %bitcast.169), calls=%async_computation.1 | async-start | bytes 8388608
  504.3 12.2 %copy-start.23 = (f32[8,1,128]{2,1,0:T(1,128)S(1)}, f32[8,1,128]{2,1,0:T(1,128)}, u32[]{:S(2)}) copy-start(f32[8,1,128]{2,1,0:T(1,128)} %get-tuple-element.134) | copy-start | bytes 12292
  504.3 12.2 %slice-start.1 = ((s8[6291456]{0:T(1024)(128)(4,1)}), s8[2097152]{0:T(1024)(128)(4,1)S(1)}, s32[]{:S(2)}) async-start(s8[6291456]{0:T(1024)(128)(4,1)} %bitcast.169), calls=%async_computation.2 | async-start | bytes 4194304
  504.3 12.2 %copy-start.29 = (bf16[1024,3072]{1,0:T(8,128)(2,1)S(1)}, bf16[1024,3072]{1,0:T(8,128)(2,1)}, u32[]{:S(2)}) copy-start(bf16[1024,3072]{1,0:T(8,128)(2,1)} %fusion.51) | copy-start | bytes 18874372
  589.9 8.9 %copy-start.22 = (bf16[128,256]{1,0:T(8,128)(2,1)S(1)}, bf16[128,256]{1,0:T(8,128)(2,1)}, u32[]{:S(2)}) copy-start(bf16[128,256]{1,0:T(8,128)(2,1)} %get-tuple-element.77) | copy-start | bytes 196612
Sparse Core Ops, SparseCore 0:
  258.6 25.9 all-gather.2
